TPU v7x, 1024 devices: a whole 4x4x32 slice. The times are simulated.
1024 devices in a mesh: dp: 64 (over x_lo, z), tensor: 16 (over x_hi, y, core).
Axes of the slice: x: 4 (x_hi: 2, x_lo: 2; x = x_hi * 2 + x_lo), y: 4, z: 32, core: 2. Of those that a mesh axis runs over, the one named last changes fastest.
Arguments:
- activations: bfloat16 [8192, 6144], P('dp'), may hold values from -3 to 3
- grad_hidden: bfloat16 [8192, 24576], P('dp', 'tensor'), may hold values from -0.59765625 to 0.59765625
- weight_tiles: bfloat16 [16, 64, 128, 128], P('tensor'), may hold values from -0.5 to 0.5
- tile_slots: int32 [16, 64], P('tensor'), may hold values from 0 to 575, as said below
- owner_map: int32 [16, 64], P('tensor'), may hold values from 0 to 63, as said below
Outputs:
- grad_input: float32 [8192, 6144], P('dp', 'tensor')
- grad_weight: float32 [64, 2048, 128], P('dp', 'tensor')
Inputs may be any that keep to these rules, and one draw needn't show every extreme that they name: `tile_slots`: each row holds 64 distinct positions in increasing order, the first being 0 and the last the largest position. `owner_map`: in each row every owner is named by exactly 1 entry.
All inputs are finite; a program needn't handle non-finite values.
Results may differ from a plain program's by a relative error of at most 0.0029.
Values sent between devices are 32-bit elements; how exact they have to be, the bound alone decides.
No kernel may reach another device: no remote copies, remote signals or barrier semaphores. Data moves between devices by JAX's collectives and lax.ppermute only.
A program may use at most 64 MiB of HBM per device.

v0:
```python
import jax
import jax.numpy as jnp
from jax import lax
from jax.sharding import PartitionSpec as P

TILE = 128


root_two_pi = 0.7978845608028654
cubic_term = 0.044715


def gelu_slope(preact):
    inner = root_two_pi * (preact + cubic_term * preact * preact * preact)
    tangent = jnp.tanh(inner)
    return 0.5 * (1.0 + tangent) + 0.5 * preact * (1.0 - tangent * tangent) * root_two_pi * (
        1.0 + 3.0 * cubic_term * preact * preact
    )


def on_device(activations, grad_hidden, weight_tiles, tile_slots, owner_map):
    owner_order = jnp.argsort(owner_map[0], stable=True)
    tiles = jnp.take(weight_tiles[0], owner_order, axis=0)
    positions = jnp.take(tile_slots[0], owner_order, axis=0)
    tok_rows = activations.shape[0]
    local_width = grad_hidden.shape[1]
    col_panels = local_width // TILE
    row_panels = activations.shape[1] // TILE
    row_index = positions // col_panels
    col_index = positions % col_panels
    x_panels = activations.reshape(tok_rows, row_panels, TILE).transpose(1, 0, 2)
    x_sel = jnp.take(x_panels, row_index, axis=0)
    pieces = jnp.einsum("ntk,nkj->ntj", x_sel, tiles, preferred_element_type=jnp.float32)
    collected = jax.ops.segment_sum(pieces, col_index, num_segments=col_panels)
    preact = collected.transpose(1, 0, 2).reshape(tok_rows, local_width)
    grad_pre = (grad_hidden.astype(jnp.float32) * gelu_slope(preact)).astype(jnp.bfloat16)
    g_panels = grad_pre.reshape(tok_rows, col_panels, TILE).transpose(1, 0, 2)
    g_sel = jnp.take(g_panels, col_index, axis=0)
    weight_grad = jnp.einsum("ntk,ntj->nkj", x_sel, g_sel, preferred_element_type=jnp.float32)
    grad_weight = lax.psum_scatter(weight_grad, "dp", scatter_dimension=0, tiled=True)
    back_rows = jnp.einsum("ntj,nkj->ntk", g_sel, tiles, preferred_element_type=jnp.float32)
    row_sums = jax.ops.segment_sum(back_rows, row_index, num_segments=row_panels)
    input_part = row_sums.transpose(1, 0, 2).reshape(tok_rows, row_panels * TILE)
    grad_input = lax.psum_scatter(input_part, "tensor", scatter_dimension=1, tiled=True)
    return (grad_input, grad_weight)


def solution(mesh):
    return jax.shard_map(
        on_device,
        mesh=mesh,
        in_specs=(
            P("dp", None),
            P("dp", "tensor"),
            P("tensor", None, None, None),
            P("tensor", None),
            P("tensor", None),
        ),
        out_specs=(P("dp", "tensor"), P("dp", "tensor", None)),
        check_vma=False,
    )
```

profile of v0, /device:TPU:6, one launch (start us, length us, event | category | flops | bytes accessed | tf_op | source)
XLA Modules:
  0.0 486.1 jit_solution(12315097343607116451)
XLA Ops:
  7.2 0.0 copy-start
  7.2 0.0 reduce-scatter.3.cloned.1.call-start
  7.2 2.8 sort.17
  10.1 1.4 gather_fusion
  11.6 2.6 copy.13
  14.2 2.6 copy.14
  16.8 0.0 copy-done
  16.8 2.1 gather_fusion.2
  18.9 3.5 gather_fusion.1
  22.4 5.0 %fusion.2 = f32[64,128,128]{2,1,0:T(8,128)} fusion(bf16[64,128,128]{2,1,0:T(8,128)(2,1)} %gather_fusion.1, pred[64]{0:T(512)(128)(4,1)S(1)} %get-tuple-element.9, bf16[64,128,128]{2,1,0:T(8,128)(2,1)} %gather_fusion.2, pred[64]{0:T(512)(128)(4,1)S(1)} %get-tuple-element.8), kind=kOutput, calls=%fused_computation.13 | convolution fusion | flops 270532608 | bytes 8388736 | tf_op jit(solution)/shard_map/ntk,nkj->ntj/dot_general | solution.py:33
  27.4 0.1 broadcast_in_dim.46
  27.5 0.0 copy-start.1
  27.5 8.8 %scatter_fusion = f32[12,128,128]{2,1,0:T(8,128)S(1)} fusion(f32[12,128,128]{2,1,0:T(8,128)S(1)} %broadcast_in_dim.46, s32[64]{0:T(128)S(1)} %get-tuple-element.7, f32[64,128,128]{2,1,0:T(8,128)} %fusion.2), kind=kCustom, calls=%fused_computation.4 | custom fusion | flops 1048576 | bytes 12583168 | tf_op jit(solution)/shard_map/scatter-add | solution.py:34
  36.3 1.1 copy.15
  37.4 0.0 copy-done.1
  37.4 0.2 copy.12
  37.6 1.7 fusion.9
  39.3 0.2 copy.16
  39.6 2.2 gather_fusion.3
  41.7 5.8 %fusion.1 = f32[64,128,128]{2,1,0:T(8,128)} fusion(bf16[64,128,128]{2,1,0:T(8,128)(2,1)} %gather_fusion.3, pred[64]{0:T(512)(128)(4,1)S(1)} %get-tuple-element.6, bf16[64,128,128]{2,1,0:T(8,128)(2,1)} %gather_fusion.2, pred[64]{0:T(512)(128)(4,1)S(1)} %get-tuple-element.8), kind=kOutput, calls=%fused_computation.12 | convolution fusion | flops 270532608 | bytes 8388736 | tf_op jit(solution)/shard_map/ntj,nkj->ntk/dot_general | solution.py:41
  47.5 2.1 broadcast_in_dim.42
  49.6 13.6 %scatter_fusion.1 = f32[48,128,128]{2,1,0:T(8,128)} fusion(f32[48,128,128]{2,1,0:T(8,128)} %broadcast_in_dim.42, s32[64]{0:T(128)S(1)} %get-tuple-element.10, f32[64,128,128]{2,1,0:T(8,128)} %fusion.1), kind=kCustom, calls=%fused_computation.5 | custom fusion | flops 1048576 | bytes 12583168 | tf_op jit(solution)/shard_map/scatter-add | solution.py:42
  63.3 3.6 copy.17
  66.8 0.0 reduce-scatter.3.cloned.1.call-update
  66.8 0.0 reduce-scatter.5.cloned.1.call-start
  66.9 5.2 %fusion = f32[64,128,128]{2,1,0:T(8,128)} fusion(bf16[64,128,128]{2,1,0:T(8,128)(2,1)} %gather_fusion.3, pred[64]{0:T(512)(128)(4,1)S(1)} %get-tuple-element.6, bf16[64,128,128]{2,1,0:T(8,128)(2,1)} %gather_fusion.1, pred[64]{0:T(512)(128)(4,1)S(1)} %get-tuple-element.9), kind=kOutput, calls=%fused_computation.11 | convolution fusion | flops 270532608 | bytes 8388736 | tf_op jit(solution)/shard_map/ntk,ntj->nkj/dot_general | solution.py:39
  72.0 0.0 reduce-scatter.5.cloned.1.call-update
  72.1 130.8 %reduce-scatter.3.cloned.1.call-done = f32[128,384]{0,1:T(8,128)} async-done(((f32[128,6144]{0,1:T(8,128)}), f32[128,384]{0,1:T(8,128)}) %reduce-scatter.3.cloned.1.call-update) | async-done | bytes 196624 | tf_op jit(solution)/shard_map/reduce_scatter | solution.py:44
  202.9 1.7 copy.19
  204.7 274.6 %reduce-scatter.5.cloned.1.call-done = f32[1,128,128]{2,1,0:T(8,128)} async-done(((f32[64,128,128]{2,1,0:T(8,128)}), f32[1,128,128]{2,1,0:T(8,128)}) %reduce-scatter.5.cloned.1.call-update) | async-done | bytes 65552 | tf_op jit(solution)/shard_map/reduce_scatter | solution.py:40
  (9 shorter events, 0.1 us)
Async XLA Ops:
  7.2 9.6 %copy-start = (bf16[1,64,128,128]{3,2,1,0:T(8,128)(2,1)S(1)}, bf16[1,64,128,128]{3,2,1,0:T(8,128)(2,1)}, u32[]{:S(2)}) copy-start(bf16[1,64,128,128]{3,2,1,0:T(8,128)(2,1)} %param.7) | copy-start | bytes 6291460
  7.2 195.7 %reduce-scatter.3.cloned.1.call-start = ((), (), s32[]{:S(2)}) async-start(), calls=%async_computation.2 | async-start | bytes 3342336 | tf_op jit(solution)/shard_map/reduce_scatter | solution.py:44
  27.5 10.0 %copy-start.1 = (bf16[128,1536]{1,0:T(8,128)(2,1)S(1)}, bf16[128,1536]{1,0:T(8,128)(2,1)}, u32[]{:S(2)}) copy-start(bf16[128,1536]{1,0:T(8,128)(2,1)} %param.6) | copy-start | bytes 1179652
  66.8 412.4 %reduce-scatter.5.cloned.1.call-start = ((), (), s32[]{:S(2)}) async-start(), calls=%async_computation.3 | async-start | bytes 4259840 | tf_op jit(solution)/shard_map/reduce_scatter | solution.py:40
Sparse Core Ops, SparseCore 0:
  67.0 135.9 reduce-scatter.2
  206.9 272.3 reduce-scatter.4
where the time goes:
time: 487 us; the launch traced here: 486 us
  waiting for transfers between devices  405 us (83%)
  other arithmetic  27 us (6%)
  local copies, waits for them, and re-layouts  23.5 us (5%)
  matrix products  15.9 us (3%)
  between operations  14.1 us (3%)
    reduce_scatter x1, waiting for transfers between devices, on_device(): lax.psum_scatter(weight_grad, 'dp', scatter_dimension=0, tiled=True)  275 us
    reduce_scatter x1, waiting for transfers between devices, on_device(): lax.psum_scatter(input_part, 'tensor', scatter_dimension=1, tiled=True)  131 us
    scatter-add x1, other arithmetic, on_device(): jax.ops.segment_sum(back_rows, row_index, num_segments=row_panels)  13.6 us
  transfers between devices with their start and end apart: 2, of which 2 were waited for; matrix products, arithmetic and copies ran while one was open for 1% of the time, Pallas kernels for 0%

commit v1 on v0

v1 whole, which is shorter than its diff:
```python
import functools

import jax
import jax.numpy as jnp
from jax import lax
from jax.experimental import pallas as pl
from jax.experimental.pallas import tpu as pltpu
from jax.sharding import PartitionSpec as P

TILE = 128
GROUP = 4
X_ROWS, X_UP = 48, 24
Z_ROWS, Z_UP = 80, 40
X_LO, X_HI, CORES = 2, 2, 2
RING = 4

root_two_pi = 0.7978845608028654
cubic_term = 0.044715


def gelu_slope(preact):
    inner = root_two_pi * (preact + cubic_term * preact * preact * preact)
    tangent = jnp.tanh(inner)
    return 0.5 * (1.0 + tangent) + 0.5 * preact * (1.0 - tangent * tangent) * root_two_pi * (
        1.0 + 3.0 * cubic_term * preact * preact
    )


def panel(index):
    return pl.ds(pl.multiple_of(index * TILE, TILE), TILE)


def weight_kernel(n_tiles, n_cols, slots, places, x_ref, g_ref, tiles_ref, gp_ref, xf_ref, up_ref, down_ref, pre_ref):
    pre_ref[...] = jnp.zeros_like(pre_ref)

    def project(step, carry):
        parts = []
        for k in range(GROUP):
            i = step * GROUP + k
            slot = slots[0, i]
            parts.append((slot % n_cols, jnp.dot(
                x_ref[:, panel(slot // n_cols)], tiles_ref[i], preferred_element_type=jnp.float32
            )))
        for col, part in parts:
            pre_ref[col] += part
        return carry

    lax.fori_loop(0, n_tiles // GROUP, project, 0)
    for col in range(n_cols):
        grad = g_ref[:, col * TILE:(col + 1) * TILE].astype(jnp.float32)
        gp_ref[col] = (grad * gelu_slope(pre_ref[col])).astype(jnp.bfloat16)

    def weight_grad(step, carry):
        for k in range(GROUP):
            i = step * GROUP + k
            slot = slots[0, i]
            part = lax.dot_general(
                x_ref[:, panel(slot // n_cols)], gp_ref[slot % n_cols],
                (((0,), (0,)), ((), ())), preferred_element_type=jnp.float32,
            )
            xf_ref[places[0, i]] = part[:X_ROWS]
            up_ref[places[1, i]] = part[X_ROWS:X_ROWS + Z_UP]
            down_ref[places[1, i]] = part[X_ROWS + Z_UP:]
        return carry

    lax.fori_loop(0, n_tiles // GROUP, weight_grad, 0)


def input_kernel(n_tiles, n_cols, slots, spots, gp_ref, tiles_ref, gi_ref):
    gi_ref[...] = jnp.zeros_like(gi_ref)

    def back(step, carry):
        parts = []
        for k in range(GROUP):
            i = step * GROUP + k
            parts.append((spots[0, i], lax.dot_general(
                gp_ref[slots[0, i] % n_cols], tiles_ref[i],
                (((1,), (1,)), ((), ())), preferred_element_type=jnp.float32,
            )))
        for spot, part in parts:
            gi_ref[spot] += part
        return carry

    lax.fori_loop(0, n_tiles // GROUP, back, 0)


def z_pairs(z_len, stride, way):
    step = [stride if (z // stride) % 2 == 0 else -stride for z in range(z_len)]
    return [(z, (z + way * step[z]) % z_len) for z in range(z_len)]


def along_z(value, z_len, pairs):
    return lax.ppermute(value, "dp", [(x * z_len + a, x * z_len + b) for x in range(X_LO) for a, b in pairs])


def swap_x(value, z_len):
    n = X_LO * z_len
    return lax.ppermute(value, "dp", [(i, (i + z_len) % n) for i in range(n)])


def halve(up, down, z_len, z, stride):
    digit = (z // stride) % 2
    half = up.shape[0] // 2
    pick = lambda value, which: lax.dynamic_slice_in_dim(value, which * half, half, 0)
    got_up = along_z(pick(up, 1 - digit), z_len, z_pairs(z_len, stride, 1))
    got_down = along_z(pick(down, 1 - digit), z_len, z_pairs(z_len, stride, -1))
    return pick(up, digit) + got_up, pick(down, digit) + got_down


def reduce_weight(xf, up, down, z_len):
    z = lax.axis_index("dp") % z_len
    n = xf.shape[0] // 4
    first_up, first_down = z_pairs(z_len, 1, 1), z_pairs(z_len, 1, -1)
    got_x = swap_x(xf[2 * n:], z_len)
    got_up = along_z(up[2 * n:], z_len, first_up)
    got_down = along_z(down[2 * n:], z_len, first_down)
    send = got_x[n:] + xf[n:2 * n]
    got_xu = along_z(send[:, :X_UP], z_len, first_up)
    got_xd = along_z(send[:, X_UP:], z_len, first_down)
    got_z = swap_x(jnp.concatenate([got_up[n:] + up[n:2 * n], got_down[n:] + down[n:2 * n]], axis=1), z_len)
    keep = got_x[:n] + xf[:n]
    up_now = jnp.concatenate([keep[:, :X_UP] + got_xu, got_up[:n] + up[:n] + got_z[:, :Z_UP]], axis=1)
    down_now = jnp.concatenate([keep[:, X_UP:] + got_xd, got_down[:n] + down[:n] + got_z[:, Z_UP:]], axis=1)
    stride = 2
    while up_now.shape[0] > RING:
        up_now, down_now = halve(up_now, down_now, z_len, z, stride)
        stride *= 2
    mine = z // stride
    chunk = lambda value, k: lax.dynamic_slice_in_dim(value, (mine + k) % RING, 1, 0)
    up_ring = [(a, (a + stride) % z_len) for a in range(z_len)]
    down_ring = [(a, (a - stride) % z_len) for a in range(z_len)]
    far_up = along_z(chunk(up_now, 2), z_len, up_ring)
    far_down = along_z(chunk(down_now, 2), z_len, down_ring)
    next_up = along_z(jnp.concatenate([chunk(up_now, 1) + far_up, chunk(down_now, 1)], axis=1), z_len, up_ring)
    next_down = along_z(jnp.concatenate([chunk(up_now, 3), chunk(down_now, 3) + far_down], axis=1), z_len, down_ring)
    total = jnp.concatenate([chunk(up_now, 0), chunk(down_now, 0)], axis=1) + next_up + next_down
    a, b, c = X_UP, X_UP + Z_UP, 2 * X_UP + Z_UP
    return jnp.concatenate([total[:, :a], total[:, b:c], total[:, a:b], total[:, c:]], axis=1)


def reduce_input(gi, n_tensor):
    y_len = n_tensor // (X_HI * CORES)
    half = gi.shape[0] // 2
    both = lax.ppermute(gi[half:], "tensor", [(i, i ^ 1) for i in range(n_tensor)]) + gi[:half]
    groups = [
        [(x * y_len + y) * CORES + c for y in range(y_len)] for x in range(X_HI) for c in range(CORES)
    ]
    part = lax.psum_scatter(both, "tensor", scatter_dimension=0, axis_index_groups=groups, tiled=True)
    last = part.shape[0] // 2
    far = n_tensor // X_HI
    return lax.ppermute(part[last:], "tensor", [(i, (i + far) % n_tensor) for i in range(n_tensor)]) + part[:last]


def on_device(n_dp, n_tensor, activations, grad_hidden, weight_tiles, tile_slots, owner_map):
    tok_rows, width = activations.shape
    n_tiles = tile_slots.shape[1]
    n_cols = grad_hidden.shape[1] // TILE
    row_panels = width // TILE
    z_len = n_dp // X_LO
    y_len = n_tensor // (X_HI * CORES)
    dp, tp = lax.axis_index("dp"), lax.axis_index("tensor")
    other_x = (owner_map // z_len) ^ (dp // z_len)
    owner_z = owner_map % z_len
    other_z = (owner_z ^ dp) & 1
    stride, chunk = 2, jnp.zeros_like(owner_z)
    while z_len // stride > RING:
        chunk = chunk * 2 + (owner_z // stride) % 2
        stride *= 2
    chunk = chunk * RING + owner_z // stride
    n = z_len // 2
    places = jnp.concatenate([other_x * 2 * n + other_z * n + chunk, other_z * 2 * n + other_x * n + chunk], axis=0)
    per = row_panels // n_tensor
    row = tile_slots // n_cols
    owner = row // per
    core, y, x_hi = owner % CORES, (owner // CORES) % y_len, owner // (CORES * y_len)
    spots = (((core ^ (tp % CORES)) * y_len + y) * X_HI + (x_hi ^ (tp // (CORES * y_len)))) * per + row % per

    vmem = pl.BlockSpec(memory_space=pltpu.VMEM)
    smem = pl.BlockSpec(memory_space=pltpu.SMEM)
    params = pltpu.CompilerParams(vmem_limit_bytes=32 * 1024 * 1024)
    flops = 2 * n_tiles * tok_rows * TILE * TILE
    gp, xf, up, down = pl.pallas_call(
        functools.partial(weight_kernel, n_tiles, n_cols),
        out_shape=(
            jax.ShapeDtypeStruct((n_cols, tok_rows, TILE), jnp.bfloat16),
            jax.ShapeDtypeStruct((n_tiles, X_ROWS, TILE), jnp.float32),
            jax.ShapeDtypeStruct((n_tiles, Z_UP, TILE), jnp.float32),
            jax.ShapeDtypeStruct((n_tiles, Z_ROWS - Z_UP, TILE), jnp.float32),
        ),
        in_specs=[smem, smem, vmem, vmem, vmem],
        out_specs=(vmem, vmem, vmem, vmem),
        scratch_shapes=[pltpu.VMEM((n_cols, tok_rows, TILE), jnp.float32)],
        compiler_params=params,
        cost_estimate=pl.CostEstimate(flops=2 * flops, bytes_accessed=8 * 2**20, transcendentals=0),
    )(tile_slots, places, activations, grad_hidden, weight_tiles[0])
    gi = pl.pallas_call(
        functools.partial(input_kernel, n_tiles, n_cols),
        out_shape=jax.ShapeDtypeStruct((row_panels, tok_rows, TILE), jnp.float32),
        in_specs=[smem, smem, vmem, vmem],
        out_specs=vmem,
        compiler_params=params,
        cost_estimate=pl.CostEstimate(flops=flops, bytes_accessed=6 * 2**20, transcendentals=0),
    )(tile_slots, spots, gp, weight_tiles[0])
    grad_weight = reduce_weight(xf, up, down, z_len)
    panels = reduce_input(gi, n_tensor)
    grad_input = panels.transpose(1, 0, 2).reshape(tok_rows, per * TILE)
    return grad_input, grad_weight


def solution(mesh):
    return jax.shard_map(
        functools.partial(on_device, mesh.shape["dp"], mesh.shape["tensor"]),
        mesh=mesh,
        in_specs=(
            P("dp", None),
            P("dp", "tensor"),
            P("tensor", None, None, None),
            P("tensor", None),
            P("tensor", None),
        ),
        out_specs=(P("dp", "tensor"), P("dp", "tensor", None)),
        check_vma=False,
    )
```

time: 487 us -> 188 us (0.39)
  waiting for transfers between devices: 405 us -> 49.5 us
  starting transfers between devices: 0.08 us -> 84.5 us
  matrix products: 15.9 us -> 0 us
  other arithmetic: 27 us -> 12.2 us
  Pallas kernels: 0 us -> 12.1 us
  local copies, waits for them, and re-layouts: 23.5 us -> 13.7 us
    reduce_scatter x2 -> x1, waiting for transfers between devices: 405 us -> 0.02 us  [reduce_input(): lax.psum_scatter(both, 'tensor', scatter_dimension=0, axis_index_groups=g...]
    ppermute x0 -> x16, starting transfers between devices: none -> 84.5 us  [the longest x12 73.6 us: along_z(): lax.ppermute(value, 'dp', [(x * z_len + a, x * z_len + b) for x in range(...]
    ppermute x0 -> x16, waiting for transfers between devices: none -> 49.5 us  [the longest x12 28.4 us: along_z(): lax.ppermute(value, 'dp', [(x * z_len + a, x * z_len + b) for x in range(...]
    scatter-add x2 -> x0, other arithmetic: 22.4 us -> none  [the longest x1 13.6 us: on_device(): jax.ops.segment_sum(back_rows, row_index, num_segments=row_panels)]
    dot_general x3 -> x0, matrix products: 15.9 us -> none  [the longest x1 5.8 us: on_device(): jnp.einsum('ntj,nkj->ntk', g_sel, tiles, preferred_element_type=jnp.float32)]
    pallas_call x0 -> x2, Pallas kernels: none -> 12.1 us  [the longest x1 7.87 us: on_device(): pl.pallas_call(functools.partial(weight_kernel, n_tiles, n_cols), out_sha...]
    add x0 -> x16, other arithmetic: none -> 9.46 us  [the longest x1 2.74 us: reduce_input(): lax.ppermute(gi[half:], 'tensor', [(i, i ^ 1) for i in range(n_tensor)])]
    gather x4 -> x0, local copies, waits for them, and re-layouts: 9.27 us -> none  [the longest x1 3.52 us: on_device(): x_sel = jnp.take(x_panels, row_index, axis=0)]
  transfers between devices with their start and end apart: 2 -> 17, of which waited for: 2 -> 10; matrix products, arithmetic and copies ran while one was open for 1% -> 7% of each run, Pallas kernels for 0% -> 2%
where the time goes in v1:
time: 188 us; the launch traced here: 187 us
  starting transfers between devices  84.5 us (45%)
  waiting for transfers between devices  49.5 us (26%)
  between operations  14.7 us (8%)
  local copies, waits for them, and re-layouts  13.7 us (7%)
  other arithmetic  12.2 us (6%)
  Pallas kernels  12.1 us (6%)
    ppermute x12, starting transfers between devices, along_z(): lax.ppermute(value, 'dp', [(x * z_len + a, x * z_len + b) for x in range(...  73.6 us
    ppermute x12, waiting for transfers between devices, along_z(): lax.ppermute(value, 'dp', [(x * z_len + a, x * z_len + b) for x in range(...  28.4 us
    ppermute x2, waiting for transfers between devices, swap_x(): return lax.ppermute(value, 'dp', [(i, (i + z_len) % n) for i in range(n)])  15.7 us
    unnamed x31, local copies, waits for them, and re-layouts  8.48 us
    pallas_call x1, Pallas kernels, on_device(): pl.pallas_call(functools.partial(weight_kernel, n_tiles, n_cols), out_sha...  7.87 us
    ppermute x2, starting transfers between devices, swap_x(): return lax.ppermute(value, 'dp', [(i, (i + z_len) % n) for i in range(n)])  5.82 us
    ppermute x1, waiting for transfers between devices, reduce_input(): lax.ppermute(part[last:], 'tensor', [(i, (i + far) % n_tensor) for i in r...  5.39 us
    pallas_call x1, Pallas kernels, on_device(): pl.pallas_call(functools.partial(input_kernel, n_tiles, n_cols), out_shap...  4.23 us
  transfers between devices with their start and end apart: 17, of which 10 were waited for; matrix products, arithmetic and copies ran while one was open for 7% of the time, Pallas kernels for 2%

profile of v1, /device:TPU:6, one launch (start us, length us, event | category | flops | bytes accessed | tf_op | source)
XLA Modules:
  0.0 186.7 jit_solution(18425218732027596486)
XLA Ops:
  7.2 0.7 add_add_fusion.1
  8.0 1.6 copy-done
  9.5 1.4 copy-done.2
  10.9 1.0 copy-done.8
  12.6 7.9 %shard_map.68 = (bf16[12,128,128]{2,1,0:T(8,128)(2,1)S(1)}, f32[64,48,128]{2,1,0:T(8,128)S(1)}, f32[64,40,128]{2,1,0:T(8,128)S(1)}, f32[64,40,128]{2,1,0:T(8,128)S(1)}) custom-call(s32[1,64]{1,0:T(1,128)S(1)} %copy-done.9, s32[2,64]{1,0:T(2,128)S(1)} %pad_add_fusion.places, bf16[128,6144]{1,0:T(8,128)(2,1)S(1)} %copy-done.2, ...), custom_call_target="tpu_custom_call" | custom-call | flops 536870912 | bytes 8388608 | tf_op jit(solution)/shard_map/pallas_call | solution.py:182
  20.5 1.0 slice.103
  21.5 18.7 %collective-permute-start.5 = (f32[32,40,128]{2,1,0:T(8,128)}, f32[32,40,128]{2,1,0:T(8,128)}, u32[]{:S(2)}, u32[]{:S(2)}) collective-permute-start(f32[32,40,128]{2,1,0:T(8,128)} %slice.103), channel_id=1, source_target_pairs={{0,496},{16,32},{32,16},{48,64},{64,48},{80,96},{96,80},{112,128},... | collective-permute-start | bytes 1966088 | tf_op jit(solution)/shard_map/ppermute | solution.py:93
  40.2 1.0 slice.91
  41.2 2.7 %collective-permute-start.2 = (f32[32,48,128]{2,1,0:T(8,128)}, f32[32,48,128]{2,1,0:T(8,128)}, u32[]{:S(2)}, u32[]{:S(2)}) collective-permute-start(f32[32,48,128]{2,1,0:T(8,128)} %slice.91), channel_id=1, source_target_pairs={{0,512},{16,528},{32,544},{48,560},{64,576},{80,592},{96,608},{112... | collective-permute-start | bytes 2359304 | tf_op jit(solution)/shard_map/ppermute | solution.py:98
  44.0 1.6 copy-done.1
  45.6 4.2 %shard_map.69 = f32[48,128,128]{2,1,0:T(8,128)S(1)} custom-call(s32[1,64]{1,0:T(1,128)S(1)} %copy-done.10, s32[1,64]{1,0:T(1,128)S(1)} %fusion.9.spots, bf16[12,128,128]{2,1,0:T(8,128)(2,1)S(1)} %get-tuple-element.6.gp_ref, bf16[64,128,128]{2,1,0:T(8,128)(2,1)S(1)} %bitcast.5), custom_call_target="tpu_custom_call" | custom-call | flops 268435456 | bytes 6291456 | tf_op jit(solution)/shard_map/pallas_call | solution.py:196
  49.8 1.3 slice.116
  51.1 2.0 %collective-permute-start = (f32[24,128,128]{2,1,0:T(8,128)}, f32[24,128,128]{2,1,0:T(8,128)}, u32[]{:S(2)}, u32[]{:S(2)}) collective-permute-start(f32[24,128,128]{2,1,0:T(8,128)} %slice.116), channel_id=1, source_target_pairs={{0,1},{1,0},{2,3},{3,2},{4,5},{5,4},{6,7},{7,6},{8,9},{9,8},{10,11... | collective-permute-start | bytes 4718600 | tf_op jit(solution)/shard_map/ppermute | solution.py:144
  53.2 1.9 %collective-permute-start.4 = (f32[32,40,128]{2,1,0:T(8,128)S(1)}, f32[32,40,128]{2,1,0:T(8,128)S(1)}, u32[]{:S(2)}, u32[]{:S(2)}) collective-permute-start(f32[32,40,128]{2,1,0:T(8,128)S(1)} %slice.98), channel_id=1, source_target_pairs={{0,16},{16,0},{32,48},{48,32},{64,80},{80,64},{96,112},{112,96},{1... | collective-permute-start | bytes 1966088 | tf_op jit(solution)/shard_map/ppermute | solution.py:93
  55.2 1.1 slice_add_fusion.6
  56.3 6.1 %collective-permute-done.2 = f32[32,48,128]{2,1,0:T(8,128)} collective-permute-done((f32[32,48,128]{2,1,0:T(8,128)}, f32[32,48,128]{2,1,0:T(8,128)}, u32[]{:S(2)}, u32[]{:S(2)}) %collective-permute-start.2) | collective-permute-done | bytes 786464 | tf_op jit(solution)/shard_map/ppermute | solution.py:98
  62.4 2.0 %slice_add_fusion.2 = (f32[16,48,128]{2,1,0:T(8,128)}, f32[16,48,128]{2,1,0:T(8,128)S(1)}) fusion(f32[32,48,128]{2,1,0:T(8,128)} %collective-permute-done.2, f32[64,48,128]{2,1,0:T(8,128)S(1)} %copy-done.4), kind=kLoop, calls=%fused_computation.11 | loop fusion | flops 196608 | bytes 2359296 | tf_op jit(solution)/shard_map/add | solution.py:121
  64.4 0.8 fusion.19
  65.2 1.9 %collective-permute-start.3 = (f32[16,24,128]{2,1,0:T(8,128)}, f32[16,24,128]{2,1,0:T(8,128)S(1)}, u32[]{:S(2)}, u32[]{:S(2)}) collective-permute-start(f32[16,24,128]{2,1,0:T(8,128)} %get-tuple-element.22), channel_id=1, source_target_pairs={{0,16},{16,0},{32,48},{48,32},{64,80},{80,64},{96,112},{112,96},{1... | collective-permute-start | bytes 589832 | tf_op jit(solution)/shard_map/ppermute | solution.py:93
  67.1 3.9 %collective-permute-start.9 = (f32[16,24,128]{2,1,0:T(8,128)}, f32[16,24,128]{2,1,0:T(8,128)S(1)}, u32[]{:S(2)}, u32[]{:S(2)}) collective-permute-start(f32[16,24,128]{2,1,0:T(8,128)} %get-tuple-element.23), channel_id=1, source_target_pairs={{0,496},{16,32},{32,16},{48,64},{64,48},{80,96},{96,80},{112,128},... | collective-permute-start | bytes 589832 | tf_op jit(solution)/shard_map/ppermute | solution.py:93
  71.0 1.6 collective-permute-done.4
  72.7 1.0 pad_maximum_fusion
  73.8 3.1 %collective-permute-start.6 = (f32[16,80,128]{2,1,0:T(8,128)}, f32[16,80,128]{2,1,0:T(8,128)}, u32[]{:S(2)}, u32[]{:S(2)}) collective-permute-start(f32[16,80,128]{2,1,0:T(8,128)} %pad_maximum_fusion), channel_id=1, source_target_pairs={{0,512},{16,528},{32,544},{48,560},{64,576},{80,592},{96,608},{112... | collective-permute-start | bytes 1966088 | tf_op jit(solution)/shard_map/ppermute | solution.py:98
  77.0 0.7 copy-done.13
  77.6 0.7 copy-done.14
  78.3 1.3 slice_add_fusion.10
  79.6 2.7 %slice_add_fusion = f32[24,128,128]{2,1,0:T(8,128)} fusion(f32[24,128,128]{2,1,0:T(8,128)} %collective-permute-done, f32[48,128,128]{2,1,0:T(8,128)S(1)} %shard_map.69), kind=kLoop, calls=%fused_computation | loop fusion | flops 393216 | bytes 4718592 | tf_op jit(solution)/shard_map/add | solution.py:144
  82.4 9.6 %collective-permute-done.6 = f32[16,80,128]{2,1,0:T(8,128)} collective-permute-done((f32[16,80,128]{2,1,0:T(8,128)}, f32[16,80,128]{2,1,0:T(8,128)}, u32[]{:S(2)}, u32[]{:S(2)}) %collective-permute-start.6) | collective-permute-done | bytes 655392 | tf_op jit(solution)/shard_map/ppermute | solution.py:98
  91.9 1.5 slice_add_fusion.5
  93.4 1.9 %collective-permute-start.7 = (f32[8,64,128]{2,1,0:T(8,128)S(1)}, f32[8,64,128]{2,1,0:T(8,128)S(1)}, u32[]{:S(2)}, u32[]{:S(2)}) collective-permute-start(f32[8,64,128]{2,1,0:T(8,128)S(1)} %fusion.3), channel_id=1, source_target_pairs={{0,32},{16,48},{32,0},{48,16},{64,96},{80,112},{96,64},{112,80},{1... | collective-permute-start | bytes 786440 | tf_op jit(solution)/shard_map/ppermute | solution.py:93
  95.6 6.0 %collective-permute-start.10 = (f32[8,64,128]{2,1,0:T(8,128)S(1)}, f32[8,64,128]{2,1,0:T(8,128)S(1)}, u32[]{:S(2)}, u32[]{:S(2)}) collective-permute-start(f32[8,64,128]{2,1,0:T(8,128)S(1)} %fusion), channel_id=1, source_target_pairs={{0,480},{16,496},{32,64},{48,80},{64,32},{80,48},{96,128},{112,144... | collective-permute-start | bytes 786440 | tf_op jit(solution)/shard_map/ppermute | solution.py:93
  101.6 6.9 %collective-permute-done.7 = f32[8,64,128]{2,1,0:T(8,128)S(1)} collective-permute-done((f32[8,64,128]{2,1,0:T(8,128)S(1)}, f32[8,64,128]{2,1,0:T(8,128)S(1)}, u32[]{:S(2)}, u32[]{:S(2)}) %collective-permute-start.7) | collective-permute-done | bytes 262176 | tf_op jit(solution)/shard_map/ppermute | solution.py:93
  108.5 1.9 %collective-permute-start.8 = (f32[4,64,128]{2,1,0:T(8,128)S(1)}, f32[4,64,128]{2,1,0:T(8,128)S(1)}, u32[]{:S(2)}, u32[]{:S(2)}) collective-permute-start(f32[4,64,128]{2,1,0:T(8,128)S(1)} %constant_dynamic-slice_fusion.7), channel_id=1, source_target_pairs={{0,64},{16,80},{32,96},{48,112},{64,0},{80,16},{96,32},{112,48},{1... | collective-permute-start | bytes 393224 | tf_op jit(solution)/shard_map/ppermute | solution.py:93
  110.5 0.8 collective-permute-done.10
  111.3 8.2 %collective-permute-start.11 = (f32[4,64,128]{2,1,0:T(8,128)S(1)}, f32[4,64,128]{2,1,0:T(8,128)S(1)}, u32[]{:S(2)}, u32[]{:S(2)}) collective-permute-start(f32[4,64,128]{2,1,0:T(8,128)S(1)} %constant_dynamic-slice_fusion.5), channel_id=1, source_target_pairs={{0,448},{16,464},{32,480},{48,496},{64,128},{80,144},{96,160},{112... | collective-permute-start | bytes 393224 | tf_op jit(solution)/shard_map/ppermute | solution.py:93
  119.5 5.6 %collective-permute-done.8 = f32[4,64,128]{2,1,0:T(8,128)S(1)} collective-permute-done((f32[4,64,128]{2,1,0:T(8,128)S(1)}, f32[4,64,128]{2,1,0:T(8,128)S(1)}, u32[]{:S(2)}, u32[]{:S(2)}) %collective-permute-start.8) | collective-permute-done | bytes 131104 | tf_op jit(solution)/shard_map/ppermute | solution.py:93
  125.2 7.3 %collective-permute-start.12 = (f32[1,64,128]{2,1,0:T(8,128)S(1)}, f32[1,64,128]{2,1,0:T(8,128)S(1)}, u32[]{:S(2)}, u32[]{:S(2)}) collective-permute-start(f32[1,64,128]{2,1,0:T(8,128)S(1)} %get-tuple-element.26), channel_id=1, source_target_pairs={{0,128},{16,144},{32,160},{48,176},{64,192},{80,208},{96,224},{112... | collective-permute-start | bytes 98312 | tf_op jit(solution)/shard_map/ppermute | solution.py:93
  132.6 7.3 %collective-permute-start.14 = (f32[1,64,128]{2,1,0:T(8,128)S(1)}, f32[1,64,128]{2,1,0:T(8,128)S(1)}, u32[]{:S(2)}, u32[]{:S(2)}) collective-permute-start(f32[1,64,128]{2,1,0:T(8,128)S(1)} %get-tuple-element.28), channel_id=1, source_target_pairs={{0,384},{16,400},{32,416},{48,432},{64,448},{80,464},{96,480},{112... | collective-permute-start | bytes 98312 | tf_op jit(solution)/shard_map/ppermute | solution.py:93
  139.8 1.2 collective-permute-done.12
  141.0 6.5 %collective-permute-start.13 = (f32[1,128,128]{2,1,0:T(8,128)S(1)}, f32[1,128,128]{2,1,0:T(8,128)S(1)}, u32[]{:S(2)}, u32[]{:S(2)}) collective-permute-start(f32[1,128,128]{2,1,0:T(8,128)S(1)} %pad_maximum_fusion.1), channel_id=1, source_target_pairs={{0,128},{16,144},{32,160},{48,176},{64,192},{80,208},{96,224},{112... | collective-permute-start | bytes 196616 | tf_op jit(solution)/shard_map/ppermute | solution.py:93
  147.6 8.1 %collective-permute-start.15 = (f32[1,128,128]{2,1,0:T(8,128)S(1)}, f32[1,128,128]{2,1,0:T(8,128)S(1)}, u32[]{:S(2)}, u32[]{:S(2)}) collective-permute-start(f32[1,128,128]{2,1,0:T(8,128)S(1)} %pad_maximum_fusion.2), channel_id=1, source_target_pairs={{0,384},{16,400},{32,416},{48,432},{64,448},{80,464},{96,480},{112... | collective-permute-start | bytes 196616 | tf_op jit(solution)/shard_map/ppermute | solution.py:93
  155.6 5.8 %collective-permute-done.13 = f32[1,128,128]{2,1,0:T(8,128)S(1)} collective-permute-done((f32[1,128,128]{2,1,0:T(8,128)S(1)}, f32[1,128,128]{2,1,0:T(8,128)S(1)}, u32[]{:S(2)}, u32[]{:S(2)}) %collective-permute-start.13) | collective-permute-done | bytes 65568 | tf_op jit(solution)/shard_map/ppermute | solution.py:93
  161.4 6.4 %collective-permute-done.15 = f32[1,128,128]{2,1,0:T(8,128)S(1)} collective-permute-done((f32[1,128,128]{2,1,0:T(8,128)S(1)}, f32[1,128,128]{2,1,0:T(8,128)S(1)}, u32[]{:S(2)}, u32[]{:S(2)}) %collective-permute-start.15) | collective-permute-done | bytes 65568 | tf_op jit(solution)/shard_map/ppermute | solution.py:93
  167.9 0.9 slice.118
  168.8 3.0 %collective-permute-start.1 = (f32[3,128,128]{2,1,0:T(8,128)S(1)}, f32[3,128,128]{2,1,0:T(8,128)S(1)}, u32[]{:S(2)}, u32[]{:S(2)}) collective-permute-start(f32[3,128,128]{2,1,0:T(8,128)S(1)} %slice.118), channel_id=1, source_target_pairs={{0,8},{1,9},{2,10},{3,11},{4,12},{5,13},{6,14},{7,15},{8,0},{9,1},... | collective-permute-start | bytes 589832 | tf_op jit(solution)/shard_map/ppermute | solution.py:151
  172.5 5.4 %collective-permute-done.1 = f32[3,128,128]{2,1,0:T(8,128)S(1)} collective-permute-done((f32[3,128,128]{2,1,0:T(8,128)S(1)}, f32[3,128,128]{2,1,0:T(8,128)S(1)}, u32[]{:S(2)}, u32[]{:S(2)}) %collective-permute-start.1) | collective-permute-done | bytes 196640 | tf_op jit(solution)/shard_map/ppermute | solution.py:151
  177.9 1.0 fusion.6
  179.0 0.8 copy.8
  (57 shorter events, 2.1 us)
Async XLA Ops:
  7.2 160.7 %reduce-scatter.2.cloned.1.call-start = ((), (), s32[]{:S(2)}) async-start(), calls=%async_computation.1 | async-start | bytes 1966080 | tf_op jit(solution)/shard_map/reduce_scatter | solution.py:148
  7.9 1.6 copy-start
  9.5 1.4 copy-start.2
  10.9 1.0 copy-start.8
  11.9 0.7 copy-start.9
  20.5 19.7 %copy-start.3 = (f32[64,48,128]{2,1,0:T(8,128)}, f32[64,48,128]{2,1,0:T(8,128)S(1)}, u32[]{:S(2)}) copy-start(f32[64,48,128]{2,1,0:T(8,128)S(1)} %get-tuple-element.7) | copy-start | bytes 4718596
  20.5 20.7 %copy-start.5 = (f32[64,40,128]{2,1,0:T(8,128)}, f32[64,40,128]{2,1,0:T(8,128)S(1)}, u32[]{:S(2)}) copy-start(f32[64,40,128]{2,1,0:T(8,128)S(1)} %get-tuple-element.8) | copy-start | bytes 3932164
  20.5 20.7 %copy-start.7 = (f32[64,40,128]{2,1,0:T(8,128)}, f32[64,40,128]{2,1,0:T(8,128)S(1)}, u32[]{:S(2)}) copy-start(f32[64,40,128]{2,1,0:T(8,128)S(1)} %get-tuple-element.9) | copy-start | bytes 3932164
  20.5 23.4 %copy-start.10 = (s32[1,64]{1,0:T(1,128)S(1)}, s32[1,64]{1,0:T(1,128)}, u32[]{:S(2)}) copy-start(s32[1,64]{1,0:T(1,128)} %slots.3) | copy-start | bytes 772
  21.5 33.7 %collective-permute-start.5 = (f32[32,40,128]{2,1,0:T(8,128)}, f32[32,40,128]{2,1,0:T(8,128)}, u32[]{:S(2)}, u32[]{:S(2)}) collective-permute-start(f32[32,40,128]{2,1,0:T(8,128)} %slice.103), channel_id=1, source_target_pairs={{0,496},{16,32},{32,16},{48,64},{64,48},{80,96},{96,80},{112,128},... | collective-permute-start | bytes 1966088 | tf_op jit(solution)/shard_map/ppermute | solution.py:93
  41.2 21.2 %collective-permute-start.2 = (f32[32,48,128]{2,1,0:T(8,128)}, f32[32,48,128]{2,1,0:T(8,128)}, u32[]{:S(2)}, u32[]{:S(2)}) collective-permute-start(f32[32,48,128]{2,1,0:T(8,128)} %slice.91), channel_id=1, source_target_pairs={{0,512},{16,528},{32,544},{48,560},{64,576},{80,592},{96,608},{112... | collective-permute-start | bytes 2359304 | tf_op jit(solution)/shard_map/ppermute | solution.py:98
  44.0 1.6 copy-start.1
  49.8 3.3 %copy-start.6 = (f32[64,40,128]{2,1,0:T(8,128)S(1)}, f32[64,40,128]{2,1,0:T(8,128)}, u32[]{:S(2)}) copy-start(f32[64,40,128]{2,1,0:T(8,128)} %copy-done.5) | copy-start | bytes 3932164
  51.1 11.3 %copy-start.4 = (f32[64,48,128]{2,1,0:T(8,128)S(1)}, f32[64,48,128]{2,1,0:T(8,128)}, u32[]{:S(2)}) copy-start(f32[64,48,128]{2,1,0:T(8,128)} %copy-done.3) | copy-start | bytes 4718596
  51.1 28.5 %collective-permute-start = (f32[24,128,128]{2,1,0:T(8,128)}, f32[24,128,128]{2,1,0:T(8,128)}, u32[]{:S(2)}, u32[]{:S(2)}) collective-permute-start(f32[24,128,128]{2,1,0:T(8,128)} %slice.116), channel_id=1, source_target_pairs={{0,1},{1,0},{2,3},{3,2},{4,5},{5,4},{6,7},{7,6},{8,9},{9,8},{10,11... | collective-permute-start | bytes 4718600 | tf_op jit(solution)/shard_map/ppermute | solution.py:144
  53.2 19.4 %collective-permute-start.4 = (f32[32,40,128]{2,1,0:T(8,128)S(1)}, f32[32,40,128]{2,1,0:T(8,128)S(1)}, u32[]{:S(2)}, u32[]{:S(2)}) collective-permute-start(f32[32,40,128]{2,1,0:T(8,128)S(1)} %slice.98), channel_id=1, source_target_pairs={{0,16},{16,0},{32,48},{48,32},{64,80},{80,64},{96,112},{112,96},{1... | collective-permute-start | bytes 1966088 | tf_op jit(solution)/shard_map/ppermute | solution.py:93
  65.2 11.8 %collective-permute-start.3 = (f32[16,24,128]{2,1,0:T(8,128)}, f32[16,24,128]{2,1,0:T(8,128)S(1)}, u32[]{:S(2)}, u32[]{:S(2)}) collective-permute-start(f32[16,24,128]{2,1,0:T(8,128)} %get-tuple-element.22), channel_id=1, source_target_pairs={{0,16},{16,0},{32,48},{48,32},{64,80},{80,64},{96,112},{112,96},{1... | collective-permute-start | bytes 589832 | tf_op jit(solution)/shard_map/ppermute | solution.py:93
  67.1 9.9 %collective-permute-start.9 = (f32[16,24,128]{2,1,0:T(8,128)}, f32[16,24,128]{2,1,0:T(8,128)S(1)}, u32[]{:S(2)}, u32[]{:S(2)}) collective-permute-start(f32[16,24,128]{2,1,0:T(8,128)} %get-tuple-element.23), channel_id=1, source_target_pairs={{0,496},{16,32},{32,16},{48,64},{64,48},{80,96},{96,80},{112,128},... | collective-permute-start | bytes 589832 | tf_op jit(solution)/shard_map/ppermute | solution.py:93
  72.6 1.1 copy-start.11
  73.8 18.2 %collective-permute-start.6 = (f32[16,80,128]{2,1,0:T(8,128)}, f32[16,80,128]{2,1,0:T(8,128)}, u32[]{:S(2)}, u32[]{:S(2)}) collective-permute-start(f32[16,80,128]{2,1,0:T(8,128)} %pad_maximum_fusion), channel_id=1, source_target_pairs={{0,512},{16,528},{32,544},{48,560},{64,576},{80,592},{96,608},{112... | collective-permute-start | bytes 1966088 | tf_op jit(solution)/shard_map/ppermute | solution.py:98
  77.0 0.7 copy-start.13
  77.6 0.7 copy-start.14
  82.3 9.6 %copy-start.12 = (f32[32,40,128]{2,1,0:T(8,128)S(1)}, f32[32,40,128]{2,1,0:T(8,128)}, u32[]{:S(2)}) copy-start(f32[32,40,128]{2,1,0:T(8,128)} %copy-done.11) | copy-start | bytes 1966084
  93.4 15.0 %collective-permute-start.7 = (f32[8,64,128]{2,1,0:T(8,128)S(1)}, f32[8,64,128]{2,1,0:T(8,128)S(1)}, u32[]{:S(2)}, u32[]{:S(2)}) collective-permute-start(f32[8,64,128]{2,1,0:T(8,128)S(1)} %fusion.3), channel_id=1, source_target_pairs={{0,32},{16,48},{32,0},{48,16},{64,96},{80,112},{96,64},{112,80},{1... | collective-permute-start | bytes 786440 | tf_op jit(solution)/shard_map/ppermute | solution.py:93
  95.6 15.7 %collective-permute-start.10 = (f32[8,64,128]{2,1,0:T(8,128)S(1)}, f32[8,64,128]{2,1,0:T(8,128)S(1)}, u32[]{:S(2)}, u32[]{:S(2)}) collective-permute-start(f32[8,64,128]{2,1,0:T(8,128)S(1)} %fusion), channel_id=1, source_target_pairs={{0,480},{16,496},{32,64},{48,80},{64,32},{80,48},{96,128},{112,144... | collective-permute-start | bytes 786440 | tf_op jit(solution)/shard_map/ppermute | solution.py:93
  108.5 16.6 %collective-permute-start.8 = (f32[4,64,128]{2,1,0:T(8,128)S(1)}, f32[4,64,128]{2,1,0:T(8,128)S(1)}, u32[]{:S(2)}, u32[]{:S(2)}) collective-permute-start(f32[4,64,128]{2,1,0:T(8,128)S(1)} %constant_dynamic-slice_fusion.7), channel_id=1, source_target_pairs={{0,64},{16,80},{32,96},{48,112},{64,0},{80,16},{96,32},{112,48},{1... | collective-permute-start | bytes 393224 | tf_op jit(solution)/shard_map/ppermute | solution.py:93
  111.3 21.2 %collective-permute-start.11 = (f32[4,64,128]{2,1,0:T(8,128)S(1)}, f32[4,64,128]{2,1,0:T(8,128)S(1)}, u32[]{:S(2)}, u32[]{:S(2)}) collective-permute-start(f32[4,64,128]{2,1,0:T(8,128)S(1)} %constant_dynamic-slice_fusion.5), channel_id=1, source_target_pairs={{0,448},{16,464},{32,480},{48,496},{64,128},{80,144},{96,160},{112... | collective-permute-start | bytes 393224 | tf_op jit(solution)/shard_map/ppermute | solution.py:93
  125.2 15.8 %collective-permute-start.12 = (f32[1,64,128]{2,1,0:T(8,128)S(1)}, f32[1,64,128]{2,1,0:T(8,128)S(1)}, u32[]{:S(2)}, u32[]{:S(2)}) collective-permute-start(f32[1,64,128]{2,1,0:T(8,128)S(1)} %get-tuple-element.26), channel_id=1, source_target_pairs={{0,128},{16,144},{32,160},{48,176},{64,192},{80,208},{96,224},{112... | collective-permute-start | bytes 98312 | tf_op jit(solution)/shard_map/ppermute | solution.py:93
  132.6 14.9 %collective-permute-start.14 = (f32[1,64,128]{2,1,0:T(8,128)S(1)}, f32[1,64,128]{2,1,0:T(8,128)S(1)}, u32[]{:S(2)}, u32[]{:S(2)}) collective-permute-start(f32[1,64,128]{2,1,0:T(8,128)S(1)} %get-tuple-element.28), channel_id=1, source_target_pairs={{0,384},{16,400},{32,416},{48,432},{64,448},{80,464},{96,480},{112... | collective-permute-start | bytes 98312 | tf_op jit(solution)/shard_map/ppermute | solution.py:93
  141.0 20.4 %collective-permute-start.13 = (f32[1,128,128]{2,1,0:T(8,128)S(1)}, f32[1,128,128]{2,1,0:T(8,128)S(1)}, u32[]{:S(2)}, u32[]{:S(2)}) collective-permute-start(f32[1,128,128]{2,1,0:T(8,128)S(1)} %pad_maximum_fusion.1), channel_id=1, source_target_pairs={{0,128},{16,144},{32,160},{48,176},{64,192},{80,208},{96,224},{112... | collective-permute-start | bytes 196616 | tf_op jit(solution)/shard_map/ppermute | solution.py:93
  147.6 20.3 %collective-permute-start.15 = (f32[1,128,128]{2,1,0:T(8,128)S(1)}, f32[1,128,128]{2,1,0:T(8,128)S(1)}, u32[]{:S(2)}, u32[]{:S(2)}) collective-permute-start(f32[1,128,128]{2,1,0:T(8,128)S(1)} %pad_maximum_fusion.2), channel_id=1, source_target_pairs={{0,384},{16,400},{32,416},{48,432},{64,448},{80,464},{96,480},{112... | collective-permute-start | bytes 196616 | tf_op jit(solution)/shard_map/ppermute | solution.py:93
  168.8 9.1 %collective-permute-start.1 = (f32[3,128,128]{2,1,0:T(8,128)S(1)}, f32[3,128,128]{2,1,0:T(8,128)S(1)}, u32[]{:S(2)}, u32[]{:S(2)}) collective-permute-start(f32[3,128,128]{2,1,0:T(8,128)S(1)} %slice.118), channel_id=1, source_target_pairs={{0,8},{1,9},{2,10},{3,11},{4,12},{5,13},{6,14},{7,15},{8,0},{9,1},... | collective-permute-start | bytes 589832 | tf_op jit(solution)/shard_map/ppermute | solution.py:151
Sparse Core Ops, SparseCore 0:
  82.5 34.8 reduce-scatter.1

commit v2 on v0

v2 whole, which is shorter than its diff:
```python
import functools

import jax
import jax.numpy as jnp
from jax import lax
from jax.experimental import pallas as pl
from jax.experimental.pallas import tpu as pltpu
from jax.sharding import PartitionSpec as P

TILE = 128
GROUP = 8
TILE_COPIES = 4
ROWS = (64, 64)
X_LO, X_HI, CORES = 2, 2, 2
RING = 8
VMEM_LIMIT = 58 * 2**20

root_two_pi = 0.7978845608028654
cubic_term = 0.044715


def gelu_slope(preact):
    inner = root_two_pi * (preact + cubic_term * preact * preact * preact)
    tangent = jnp.tanh(inner)
    return 0.5 * (1.0 + tangent) + 0.5 * preact * (1.0 - tangent * tangent) * root_two_pi * (
        1.0 + 3.0 * cubic_term * preact * preact
    )


def panel(index):
    return pl.ds(pl.multiple_of(index * TILE, TILE), TILE)


def tile_place(owner, here, z_len):
    other_x = (owner // z_len) ^ (here // z_len)
    owner_z = owner % z_len
    other_z = (owner_z ^ here) & 1
    stride, chunk = 2, 0
    while z_len // stride > RING:
        chunk = chunk * 2 + (owner_z // stride) % 2
        stride *= 2
    return (other_z * 2 + other_x) * (z_len // 2) + chunk * RING + owner_z // stride


def tile_copies(tiles_hbm, tiles_ref, sems):
    n = tiles_ref.shape[0] // TILE_COPIES
    return [
        pltpu.make_async_copy(tiles_hbm.at[pl.ds(k * n, n)], tiles_ref.at[pl.ds(k * n, n)], sems.at[k])
        for k in range(TILE_COPIES)
    ]


def tile_kernel(
    n_tiles, n_cols, per, z_len, y_len, slots_hbm, owners_hbm, x_hbm, g_hbm, tiles_hbm, send_hbm, keep_hbm, *refs
):
    outs, refs = refs[:2 * len(ROWS)], refs[2 * len(ROWS):]
    x_ref, g_ref, tiles_ref, pre_ref, gp_ref, gi_ref, slots, owners, order, sems = refs
    x_copy = pltpu.make_async_copy(x_hbm, x_ref, sems.at[TILE_COPIES])
    g_copy = pltpu.make_async_copy(g_hbm, g_ref, sems.at[TILE_COPIES + 1])
    scalars = [
        pltpu.make_async_copy(slots_hbm, slots, sems.at[TILE_COPIES + 2]),
        pltpu.make_async_copy(owners_hbm, owners, sems.at[TILE_COPIES + 3]),
    ]
    arriving = tile_copies(tiles_hbm, tiles_ref, sems)
    for copy in (*scalars, x_copy, *arriving, g_copy):
        copy.start()
    pre_ref[...] = jnp.zeros_like(pre_ref)
    gi_ref[...] = jnp.zeros_like(gi_ref)
    here = lax.axis_index("dp")
    for copy in scalars:
        copy.wait()

    def note(i, carry):
        order[tile_place(owners[0, i], here, z_len)] = i
        return carry

    lax.fori_loop(0, n_tiles, note, 0)
    x_copy.wait()

    def project(step, carry):
        products = []
        for k in range(GROUP):
            i = step * GROUP + k
            slot = slots[0, i]
            products.append((slot % n_cols, jnp.dot(
                x_ref[:, panel(slot // n_cols)], tiles_ref[i], preferred_element_type=jnp.float32
            )))
        for col, product in products:
            pre_ref[col] += product
        return carry

    steps = n_tiles // TILE_COPIES // GROUP
    for k in range(TILE_COPIES):
        arriving[k].wait()
        lax.fori_loop(k * steps, (k + 1) * steps, project, 0)
    g_copy.wait()
    for col in range(n_cols):
        grad = g_ref[:, col * TILE:(col + 1) * TILE].astype(jnp.float32)
        gp_ref[col] = (grad * gelu_slope(pre_ref[col])).astype(jnp.bfloat16)

    near = lax.axis_index("tensor")

    def back(step, carry):
        products = []
        for k in range(GROUP):
            i = step * GROUP + k
            row = slots[0, i] // n_cols
            owner = row // per
            core, y, x_hi = owner % CORES, (owner // CORES) % y_len, owner // (CORES * y_len)
            core, x_hi = core ^ (near % CORES), x_hi ^ (near // (CORES * y_len))
            products.append((((core * y_len + y) * X_HI + x_hi) * per + row % per, lax.dot_general(
                gp_ref[slots[0, i] % n_cols], tiles_ref[i],
                (((1,), (1,)), ((), ())), preferred_element_type=jnp.float32,
            )))
        for spot, product in products:
            gi_ref[spot] += product
        return carry

    lax.fori_loop(0, n_tiles // GROUP, back, 0)
    half = gi_ref.shape[0] // 2
    leaving = [
        pltpu.make_async_copy(gi_ref.at[pl.ds(half, half)], send_hbm, sems.at[TILE_COPIES + 4]),
        pltpu.make_async_copy(gi_ref.at[pl.ds(0, half)], keep_hbm, sems.at[TILE_COPIES + 5]),
    ]
    for copy in leaving:
        copy.start()

    n = z_len // 2
    for kind in range(4):
        other_z, other_x = kind // 2, kind % 2

        def weight_grad(step, carry):
            for k in range(GROUP):
                place = kind * n + step * GROUP + k
                slot = slots[0, order[place]]
                product = lax.dot_general(
                    x_ref[:, panel(slot // n_cols)], gp_ref[slot % n_cols],
                    (((0,), (0,)), ((), ())), preferred_element_type=jnp.float32,
                )
                start = 0
                for p, rows in enumerate(ROWS):
                    outs[2 * p + other_z][other_x * n + step * GROUP + k] = product[start:start + rows]
                    start += rows
            return carry

        lax.fori_loop(0, n // GROUP, weight_grad, 0)
    for copy in leaving:
        copy.wait()


def along_z(value, sizes, move):
    n_dp, n_tensor = sizes
    z_len = n_dp // X_LO
    pairs = []
    for dp in range(n_dp):
        for tp in range(n_tensor):
            z = move(dp % z_len, tp % CORES) % z_len
            pairs.append((dp * n_tensor + tp, (dp - dp % z_len + z) * n_tensor + tp))
    return lax.ppermute(value, ("dp", "tensor"), pairs)


def partner(stride):
    return lambda z, core: z + stride * (1 - 2 * ((z // stride + core) % 2))


def swap_x(value, sizes):
    n_dp = sizes[0]
    return lax.ppermute(value, "dp", [(i, (i + n_dp // X_LO) % n_dp) for i in range(n_dp)])


def pick(value, at, count):
    return lax.dynamic_slice_in_dim(value, at * count, count, 0)


def swap_cores(value, sizes):
    return lax.ppermute(value, "tensor", [(i, i ^ 1) for i in range(sizes[1])])


def swap_x_hi(value, sizes):
    n_tensor = sizes[1]
    return lax.ppermute(value, "tensor", [(i, (i + n_tensor // X_HI) % n_tensor) for i in range(n_tensor)])


def sum_over_y(value, sizes):
    y_len = sizes[1] // (X_HI * CORES)
    groups = [
        [(x * y_len + y) * CORES + c for y in range(y_len)] for x in range(X_HI) for c in range(CORES)
    ]
    return lax.psum_scatter(value, "tensor", scatter_dimension=0, axis_index_groups=groups, tiled=True)


def reduce_all(parts, send, keep, sizes):
    z = lax.rem(lax.axis_index("dp"), sizes[0] // X_LO)
    core = lax.rem(lax.axis_index("tensor"), CORES)
    got_parts = [along_z(away, sizes, partner(1)) for away, _ in parts]
    panels = sum_over_y(swap_cores(send, sizes) + keep, sizes)
    sums = []
    for got, (_, here) in zip(got_parts, parts):
        n = got.shape[0] // 2
        now = got[:n] + here[:n] + swap_x(got[n:] + here[n:], sizes)
        stride = 2
        while now.shape[0] > RING:
            half, digit = now.shape[0] // 2, lax.rem(lax.div(z, stride), 2)
            now = pick(now, digit, half) + along_z(pick(now, 1 - digit, half), sizes, partner(stride))
            stride *= 2
        sums.append(now)
    now = jnp.concatenate(sums, axis=1)
    mine, way = lax.div(z, stride), 1 - 2 * core
    chunk = lambda k: pick(now, lax.rem(mine + k * way + RING, RING), 1)
    far, near, total = chunk(RING // 2), None, chunk(0)
    for k in range(RING // 2, 0, -1):
        if near is not None:
            far, near = lax.optimization_barrier((far, near))
        far = along_z(far, sizes, lambda z, core: z + stride * (1 - 2 * core))
        if near is not None:
            near = along_z(near, sizes, lambda z, core: z - stride * (1 - 2 * core))
        if k > 1:
            far = far + chunk(k - 1)
            near = chunk(1 - k) if near is None else near + chunk(1 - k)
    half = panels.shape[0] // 2
    panels = swap_x_hi(panels[half:], sizes) + panels[:half]
    return jnp.concatenate([panels[j] for j in range(half)], axis=1), total + far + near


def on_device(n_dp, n_tensor, activations, grad_hidden, weight_tiles, tile_slots, owner_map):
    tok_rows, width = activations.shape
    n_tiles = tile_slots.shape[1]
    n_cols = grad_hidden.shape[1] // TILE
    row_panels = width // TILE
    per = row_panels // n_tensor
    z_len = n_dp // X_LO
    y_len = n_tensor // (X_HI * CORES)
    hbm = pl.BlockSpec(memory_space=pl.ANY)
    vmem = pl.BlockSpec(memory_space=pltpu.VMEM)
    flops = 2 * n_tiles * tok_rows * TILE * TILE
    f32 = lambda *shape: jax.ShapeDtypeStruct(shape, jnp.float32)
    f32_parts = [f32(n_tiles // 2, rows, TILE) for rows in ROWS for _ in range(2)]
    send, keep, *parts = pl.pallas_call(
        functools.partial(tile_kernel, n_tiles, n_cols, per, z_len, y_len),
        out_shape=(f32(row_panels // 2, tok_rows, TILE), f32(row_panels // 2, tok_rows, TILE), *f32_parts),
        in_specs=[hbm] * 5,
        out_specs=(hbm, hbm) + (vmem,) * len(f32_parts),
        scratch_shapes=[
            pltpu.VMEM(activations.shape, jnp.bfloat16),
            pltpu.VMEM(grad_hidden.shape, jnp.bfloat16),
            pltpu.VMEM((n_tiles, TILE, TILE), jnp.bfloat16),
            pltpu.VMEM((n_cols, tok_rows, TILE), jnp.float32),
            pltpu.VMEM((n_cols, tok_rows, TILE), jnp.bfloat16),
            pltpu.VMEM((row_panels, tok_rows, TILE), jnp.float32),
            pltpu.SMEM((1, n_tiles), jnp.int32),
            pltpu.SMEM((1, n_tiles), jnp.int32),
            pltpu.SMEM((n_tiles,), jnp.int32),
            pltpu.SemaphoreType.DMA((6 + TILE_COPIES,)),
        ],
        compiler_params=pltpu.CompilerParams(vmem_limit_bytes=VMEM_LIMIT),
        cost_estimate=pl.CostEstimate(flops=3 * flops, bytes_accessed=12 * 2**20, transcendentals=0),
    )(tile_slots, owner_map, activations, grad_hidden, weight_tiles[0])
    pairs = [(parts[2 * p + 1], parts[2 * p]) for p in range(len(ROWS))]
    return reduce_all(pairs, send, keep, (n_dp, n_tensor))


def solution(mesh):
    return jax.shard_map(
        functools.partial(on_device, mesh.shape["dp"], mesh.shape["tensor"]),
        mesh=mesh,
        in_specs=(
            P("dp", None),
            P("dp", "tensor"),
            P("tensor", None, None, None),
            P("tensor", None),
            P("tensor", None),
        ),
        out_specs=(P("dp", "tensor"), P("dp", "tensor", None)),
        check_vma=False,
    )
```

time: 487 us -> 165 us (0.34)
  waiting for transfers between devices: 405 us -> 52.4 us
  starting transfers between devices: 0.08 us -> 73.1 us
  local copies, waits for them, and re-layouts: 23.5 us -> 1.01 us
  other arithmetic: 27 us -> 10.1 us
  matrix products: 15.9 us -> 0 us
  Pallas kernels: 0 us -> 12.1 us
    reduce_scatter x2 -> x1, waiting for transfers between devices: 405 us -> 0.02 us  [sum_over_y(): lax.psum_scatter(value, 'tensor', scatter_dimension=0, axis_index_groups=...]
    ppermute x0 -> x15, starting transfers between devices: none -> 73.1 us  [the longest x11 62.4 us: along_z(): return lax.ppermute(value, ('dp', 'tensor'), pairs)]
    ppermute x0 -> x15, waiting for transfers between devices: none -> 52.3 us  [the longest x11 46.9 us: along_z(): return lax.ppermute(value, ('dp', 'tensor'), pairs)]
    scatter-add x2 -> x0, other arithmetic: 22.4 us -> none  [the longest x1 13.6 us: on_device(): jax.ops.segment_sum(back_rows, row_index, num_segments=row_panels)]
    dot_general x3 -> x0, matrix products: 15.9 us -> none  [the longest x1 5.8 us: on_device(): jnp.einsum('ntj,nkj->ntk', g_sel, tiles, preferred_element_type=jnp.float32)]
    pallas_call x0 -> x1, Pallas kernels: none -> 12.1 us  [on_device(): pl.pallas_call(functools.partial(tile_kernel, n_tiles, n_cols, per, z_len...]
    add x0 -> x12, other arithmetic: none -> 9.35 us  [the longest x4 3.89 us: reduce_all(): now = got[:n] + here[:n] + swap_x(got[n:] + here[n:], sizes)]
    gather x4 -> x0, local copies, waits for them, and re-layouts: 9.27 us -> none  [the longest x1 3.52 us: on_device(): x_sel = jnp.take(x_panels, row_index, axis=0)]
  transfers between devices with their start and end apart: 2 -> 16, of which waited for: 2 -> 10; matrix products, arithmetic and copies ran while one was open for 1% -> 6% of each run, Pallas kernels for 0% -> 0%
where the time goes in v2:
time: 165 us; the launch traced here: 163 us
  starting transfers between devices  73.1 us (44%)
  waiting for transfers between devices  52.4 us (32%)
  between operations  14.5 us (9%)
  Pallas kernels  12.1 us (7%)
  other arithmetic  10.1 us (6%)
    ppermute x11, starting transfers between devices, along_z(): return lax.ppermute(value, ('dp', 'tensor'), pairs)  62.4 us
    ppermute x11, waiting for transfers between devices, along_z(): return lax.ppermute(value, ('dp', 'tensor'), pairs)  46.9 us
    pallas_call x1, Pallas kernels, on_device(): pl.pallas_call(functools.partial(tile_kernel, n_tiles, n_cols, per, z_len...  12.1 us
    ppermute x1, waiting for transfers between devices, swap_x_hi(): lax.ppermute(value, 'tensor', [(i, (i + n_tensor // X_HI) % n_tensor) for...  5.48 us
    ppermute x2, starting transfers between devices, swap_x(): lax.ppermute(value, 'dp', [(i, (i + n_dp // X_LO) % n_dp) for i in range(...  5.46 us
    add x4, other arithmetic, reduce_all(): now = got[:n] + here[:n] + swap_x(got[n:] + here[n:], sizes)  3.89 us
    ppermute x1, starting transfers between devices, swap_x_hi(): lax.ppermute(value, 'tensor', [(i, (i + n_tensor // X_HI) % n_tensor) for...  3.32 us
  transfers between devices with their start and end apart: 16, of which 10 were waited for; matrix products, arithmetic and copies ran while one was open for 6% of the time, Pallas kernels for 0%

profile of v2, /device:TPU:6, one launch (start us, length us, event | category | flops | bytes accessed | tf_op | source)
XLA Modules:
  0.0 163.1 jit_solution(15072064463185639659)
XLA Ops:
  7.2 0.0 reduce-scatter.2.cloned.1.call-start
  7.2 12.1 %shard_map.68 = (f32[24,128,128]{2,1,0:T(8,128)}, f32[24,128,128]{2,1,0:T(8,128)}, f32[32,64,128]{2,1,0:T(8,128)}, f32[32,64,128]{2,1,0:T(8,128)}, f32[32,64,128]{2,1,0:T(8,128)}, /*index=5*/f32[32,64,128]{2,1,0:T(8,128)}) custom-call(s32[1,64]{1,0:T(1,128)} %slots_hbm.1, s32[1,64]{1,0:T(1,128)} %owners_hbm.1, bf16[128,6144]{1,0:T(8,128)(2,1)} %x_hbm.1, ...), custom_call_target="tpu_custom_call" | custom-call | flops 805306368 | bytes 12582912 | tf_op jit(solution)/shard_map/pallas_call | solution.py:238
  19.3 1.9 %collective-permute-start = (f32[24,128,128]{2,1,0:T(8,128)}, f32[24,128,128]{2,1,0:T(8,128)S(1)}, u32[]{:S(2)}, u32[]{:S(2)}) collective-permute-start(f32[24,128,128]{2,1,0:T(8,128)} %get-tuple-element.14), channel_id=1, source_target_pairs={{0,1},{1,0},{2,3},{3,2},{4,5},{5,4},{6,7},{7,6},{8,9},{9,8},{10,11... | collective-permute-start | bytes 4718600 | tf_op jit(solution)/shard_map/ppermute | solution.py:176
  21.2 3.8 %collective-permute-start.5 = (f32[32,64,128]{2,1,0:T(8,128)}, f32[32,64,128]{2,1,0:T(8,128)}, u32[]{:S(2)}, u32[]{:S(2)}) collective-permute-start(f32[32,64,128]{2,1,0:T(8,128)} %get-tuple-element.18), channel_id=1, source_target_pairs={{0,16},{1,497},{2,18},{3,499},{4,20},{5,501},{6,22},{7,503},{8,24}... | collective-permute-start | bytes 3145736 | tf_op jit(solution)/shard_map/ppermute | solution.py:159
  25.1 2.0 %collective-permute-start.2 = (f32[32,64,128]{2,1,0:T(8,128)}, f32[32,64,128]{2,1,0:T(8,128)S(1)}, u32[]{:S(2)}, u32[]{:S(2)}) collective-permute-start(f32[32,64,128]{2,1,0:T(8,128)} %get-tuple-element.16), channel_id=1, source_target_pairs={{0,16},{1,497},{2,18},{3,499},{4,20},{5,501},{6,22},{7,503},{8,24}... | collective-permute-start | bytes 3145736 | tf_op jit(solution)/shard_map/ppermute | solution.py:159
  27.1 0.0 collective-permute-done
  27.1 2.8 %add.130 = f32[24,128,128]{2,1,0:T(8,128)} add(f32[24,128,128]{2,1,0:T(8,128)S(1)} %collective-permute-done, f32[24,128,128]{2,1,0:T(8,128)} %get-tuple-element.15) | non-fusion elementwise | flops 393216 | bytes 4718592 | tf_op jit(solution)/shard_map/add | solution.py:196
  29.9 0.0 copy-start
  29.9 0.0 reduce-scatter.2.cloned.1.call-update
  29.9 8.3 %collective-permute-done.5 = f32[32,64,128]{2,1,0:T(8,128)} collective-permute-done((f32[32,64,128]{2,1,0:T(8,128)}, f32[32,64,128]{2,1,0:T(8,128)}, u32[]{:S(2)}, u32[]{:S(2)}) %collective-permute-start.5) | collective-permute-done | bytes 1048608 | tf_op jit(solution)/shard_map/ppermute | solution.py:159
  38.2 1.3 slice_add_fusion
  39.5 2.7 %collective-permute-start.6 = (f32[16,64,128]{2,1,0:T(8,128)S(1)}, f32[16,64,128]{2,1,0:T(8,128)}, u32[]{:S(2)}, u32[]{:S(2)}) collective-permute-start(f32[16,64,128]{2,1,0:T(8,128)S(1)} %slice_add_fusion), channel_id=1, source_target_pairs={{0,512},{16,528},{32,544},{48,560},{64,576},{80,592},{96,608},{112... | collective-permute-start | bytes 1572872 | tf_op jit(solution)/shard_map/ppermute | solution.py:168
  42.2 7.1 %collective-permute-done.2 = f32[32,64,128]{2,1,0:T(8,128)S(1)} collective-permute-done((f32[32,64,128]{2,1,0:T(8,128)}, f32[32,64,128]{2,1,0:T(8,128)S(1)}, u32[]{:S(2)}, u32[]{:S(2)}) %collective-permute-start.2) | collective-permute-done | bytes 1048608 | tf_op jit(solution)/shard_map/ppermute | solution.py:159
  49.4 0.0 copy-done
  49.4 0.1 slice_add_fusion.2
  49.4 2.7 %collective-permute-start.3 = (f32[16,64,128]{2,1,0:T(8,128)S(1)}, f32[16,64,128]{2,1,0:T(8,128)}, u32[]{:S(2)}, u32[]{:S(2)}) collective-permute-start(f32[16,64,128]{2,1,0:T(8,128)S(1)} %slice_add_fusion.2), channel_id=1, source_target_pairs={{0,512},{16,528},{32,544},{48,560},{64,576},{80,592},{96,608},{112... | collective-permute-start | bytes 1572872 | tf_op jit(solution)/shard_map/ppermute | solution.py:168
  52.2 0.0 collective-permute-done.6
  52.2 1.4 fusion
  53.7 9.1 %collective-permute-start.7 = (f32[8,64,128]{2,1,0:T(8,128)S(1)}, f32[8,64,128]{2,1,0:T(8,128)}, u32[]{:S(2)}, u32[]{:S(2)}) collective-permute-start(f32[8,64,128]{2,1,0:T(8,128)S(1)} %constant_dynamic-slice_fusion), channel_id=1, source_target_pairs={{0,32},{1,481},{2,34},{3,483},{4,36},{5,485},{6,38},{7,487},{8,40}... | collective-permute-start | bytes 786440 | tf_op jit(solution)/shard_map/ppermute | solution.py:159
  62.8 0.0 collective-permute-done.3
  62.8 1.1 fusion.1
  63.9 8.6 %collective-permute-start.4 = (f32[8,64,128]{2,1,0:T(8,128)S(1)}, f32[8,64,128]{2,1,0:T(8,128)S(1)}, u32[]{:S(2)}, u32[]{:S(2)}) collective-permute-start(f32[8,64,128]{2,1,0:T(8,128)S(1)} %constant_dynamic-slice_fusion.1), channel_id=1, source_target_pairs={{0,32},{1,481},{2,34},{3,483},{4,36},{5,485},{6,38},{7,487},{8,40}... | collective-permute-start | bytes 786440 | tf_op jit(solution)/shard_map/ppermute | solution.py:159
  72.6 0.0 collective-permute-done.7
  72.6 1.0 dynamic-slice_add_fusion
  73.6 4.9 %collective-permute-done.4 = f32[8,64,128]{2,1,0:T(8,128)S(1)} collective-permute-done((f32[8,64,128]{2,1,0:T(8,128)S(1)}, f32[8,64,128]{2,1,0:T(8,128)S(1)}, u32[]{:S(2)}, u32[]{:S(2)}) %collective-permute-start.4) | collective-permute-done | bytes 262176 | tf_op jit(solution)/shard_map/ppermute | solution.py:159
  78.6 9.6 %collective-permute-start.8 = (f32[1,128,128]{2,1,0:T(8,128)S(1)}, f32[1,128,128]{2,1,0:T(8,128)S(1)}, u32[]{:S(2)}, u32[]{:S(2)}) collective-permute-start(f32[1,128,128]{2,1,0:T(8,128)S(1)} %get-tuple-element.31), channel_id=1, source_target_pairs={{0,64},{1,449},{2,66},{3,451},{4,68},{5,453},{6,70},{7,455},{8,72}... | collective-permute-start | bytes 196616 | tf_op jit(solution)/shard_map/ppermute | solution.py:159
  88.2 14.3 %collective-permute-done.8 = f32[1,128,128]{2,1,0:T(8,128)S(1)} collective-permute-done((f32[1,128,128]{2,1,0:T(8,128)S(1)}, f32[1,128,128]{2,1,0:T(8,128)S(1)}, u32[]{:S(2)}, u32[]{:S(2)}) %collective-permute-start.8) | collective-permute-done | bytes 65568 | tf_op jit(solution)/shard_map/ppermute | solution.py:159
  102.5 7.8 %collective-permute-start.10 = (f32[1,128,128]{2,1,0:T(8,128)S(1)}, f32[1,128,128]{2,1,0:T(8,128)S(1)}, u32[]{:S(2)}, u32[]{:S(2)}) collective-permute-start(f32[1,128,128]{2,1,0:T(8,128)S(1)} %get-tuple-element.21), channel_id=1, source_target_pairs={{0,448},{1,65},{2,450},{3,67},{4,452},{5,69},{6,454},{7,71},{8,456... | collective-permute-start | bytes 196616 | tf_op jit(solution)/shard_map/ppermute | solution.py:159
  110.4 1.9 %collective-permute-start.9 = (f32[1,128,128]{2,1,0:T(8,128)S(1)}, f32[1,128,128]{2,1,0:T(8,128)S(1)}, u32[]{:S(2)}, u32[]{:S(2)}) collective-permute-start(f32[1,128,128]{2,1,0:T(8,128)S(1)} %fusion.9), channel_id=1, source_target_pairs={{0,64},{1,449},{2,66},{3,451},{4,68},{5,453},{6,70},{7,455},{8,72}... | collective-permute-start | bytes 196616 | tf_op jit(solution)/shard_map/ppermute | solution.py:159
  112.3 4.2 %collective-permute-done.10 = f32[1,128,128]{2,1,0:T(8,128)S(1)} collective-permute-done((f32[1,128,128]{2,1,0:T(8,128)S(1)}, f32[1,128,128]{2,1,0:T(8,128)S(1)}, u32[]{:S(2)}, u32[]{:S(2)}) %collective-permute-start.10) | collective-permute-done | bytes 65568 | tf_op jit(solution)/shard_map/ppermute | solution.py:159
  116.5 4.0 %collective-permute-done.9 = f32[1,128,128]{2,1,0:T(8,128)S(1)} collective-permute-done((f32[1,128,128]{2,1,0:T(8,128)S(1)}, f32[1,128,128]{2,1,0:T(8,128)S(1)}, u32[]{:S(2)}, u32[]{:S(2)}) %collective-permute-start.9) | collective-permute-done | bytes 65568 | tf_op jit(solution)/shard_map/ppermute | solution.py:159
  120.5 1.9 %collective-permute-start.11 = (f32[1,128,128]{2,1,0:T(8,128)S(1)}, f32[1,128,128]{2,1,0:T(8,128)S(1)}, u32[]{:S(2)}, u32[]{:S(2)}) collective-permute-start(f32[1,128,128]{2,1,0:T(8,128)S(1)} %get-tuple-element.22), channel_id=1, source_target_pairs={{0,64},{1,449},{2,66},{3,451},{4,68},{5,453},{6,70},{7,455},{8,72}... | collective-permute-start | bytes 196616 | tf_op jit(solution)/shard_map/ppermute | solution.py:159
  122.5 7.8 %collective-permute-start.12 = (f32[1,128,128]{2,1,0:T(8,128)S(1)}, f32[1,128,128]{2,1,0:T(8,128)S(1)}, u32[]{:S(2)}, u32[]{:S(2)}) collective-permute-start(f32[1,128,128]{2,1,0:T(8,128)S(1)} %get-tuple-element.23), channel_id=1, source_target_pairs={{0,448},{1,65},{2,450},{3,67},{4,452},{5,69},{6,454},{7,71},{8,456... | collective-permute-start | bytes 196616 | tf_op jit(solution)/shard_map/ppermute | solution.py:159
  130.3 0.3 collective-permute-done.11
  130.6 2.5 %collective-permute-done.12 = f32[1,128,128]{2,1,0:T(8,128)S(1)} collective-permute-done((f32[1,128,128]{2,1,0:T(8,128)S(1)}, f32[1,128,128]{2,1,0:T(8,128)S(1)}, u32[]{:S(2)}, u32[]{:S(2)}) %collective-permute-start.12) | collective-permute-done | bytes 65568 | tf_op jit(solution)/shard_map/ppermute | solution.py:159
  133.2 3.2 %collective-permute-start.13 = (f32[1,128,128]{2,1,0:T(8,128)S(1)}, f32[1,128,128]{2,1,0:T(8,128)S(1)}, u32[]{:S(2)}, u32[]{:S(2)}) collective-permute-start(f32[1,128,128]{2,1,0:T(8,128)S(1)} %get-tuple-element.24), channel_id=1, source_target_pairs={{0,64},{1,449},{2,66},{3,451},{4,68},{5,453},{6,70},{7,455},{8,72}... | collective-permute-start | bytes 196616 | tf_op jit(solution)/shard_map/ppermute | solution.py:159
  136.5 6.6 %collective-permute-start.14 = (f32[1,128,128]{2,1,0:T(8,128)S(1)}, f32[1,128,128]{2,1,0:T(8,128)S(1)}, u32[]{:S(2)}, u32[]{:S(2)}) collective-permute-start(f32[1,128,128]{2,1,0:T(8,128)S(1)} %get-tuple-element.25), channel_id=1, source_target_pairs={{0,448},{1,65},{2,450},{3,67},{4,452},{5,69},{6,454},{7,71},{8,456... | collective-permute-start | bytes 196616 | tf_op jit(solution)/shard_map/ppermute | solution.py:159
  143.0 0.0 reduce-scatter.2.cloned.1.call-done
  143.1 0.9 slice.52
  144.0 3.3 %collective-permute-start.1 = (f32[3,128,128]{2,1,0:T(8,128)S(1)}, f32[3,128,128]{2,1,0:T(8,128)S(1)}, u32[]{:S(2)}, u32[]{:S(2)}) collective-permute-start(f32[3,128,128]{2,1,0:T(8,128)S(1)} %slice.52), channel_id=1, source_target_pairs={{0,8},{1,9},{2,10},{3,11},{4,12},{5,13},{6,14},{7,15},{8,0},{9,1},... | collective-permute-start | bytes 589832 | tf_op jit(solution)/shard_map/ppermute | solution.py:181
  147.3 0.0 collective-permute-done.13
  147.3 1.2 collective-permute-done.14
  148.5 0.6 fusion.6
  149.1 5.5 %collective-permute-done.1 = f32[3,128,128]{2,1,0:T(8,128)S(1)} collective-permute-done((f32[3,128,128]{2,1,0:T(8,128)S(1)}, f32[3,128,128]{2,1,0:T(8,128)S(1)}, u32[]{:S(2)}, u32[]{:S(2)}) %collective-permute-start.1) | collective-permute-done | bytes 196640 | tf_op jit(solution)/shard_map/ppermute | solution.py:181
  154.6 1.0 slice_add_fusion.4
  155.6 0.7 pad_maximum_fusion
  (8 shorter events, 0.2 us)
Async XLA Ops:
  7.2 135.9 %reduce-scatter.2.cloned.1.call-start = ((), (), s32[]{:S(2)}) async-start(), calls=%async_computation.1 | async-start | bytes 1966080 | tf_op jit(solution)/shard_map/reduce_scatter | solution.py:189
  19.3 7.8 %collective-permute-start = (f32[24,128,128]{2,1,0:T(8,128)}, f32[24,128,128]{2,1,0:T(8,128)S(1)}, u32[]{:S(2)}, u32[]{:S(2)}) collective-permute-start(f32[24,128,128]{2,1,0:T(8,128)} %get-tuple-element.14), channel_id=1, source_target_pairs={{0,1},{1,0},{2,3},{3,2},{4,5},{5,4},{6,7},{7,6},{8,9},{9,8},{10,11... | collective-permute-start | bytes 4718600 | tf_op jit(solution)/shard_map/ppermute | solution.py:176
  21.2 17.0 %collective-permute-start.5 = (f32[32,64,128]{2,1,0:T(8,128)}, f32[32,64,128]{2,1,0:T(8,128)}, u32[]{:S(2)}, u32[]{:S(2)}) collective-permute-start(f32[32,64,128]{2,1,0:T(8,128)} %get-tuple-element.18), channel_id=1, source_target_pairs={{0,16},{1,497},{2,18},{3,499},{4,20},{5,501},{6,22},{7,503},{8,24}... | collective-permute-start | bytes 3145736 | tf_op jit(solution)/shard_map/ppermute | solution.py:159
  25.1 24.3 %collective-permute-start.2 = (f32[32,64,128]{2,1,0:T(8,128)}, f32[32,64,128]{2,1,0:T(8,128)S(1)}, u32[]{:S(2)}, u32[]{:S(2)}) collective-permute-start(f32[32,64,128]{2,1,0:T(8,128)} %get-tuple-element.16), channel_id=1, source_target_pairs={{0,16},{1,497},{2,18},{3,499},{4,20},{5,501},{6,22},{7,503},{8,24}... | collective-permute-start | bytes 3145736 | tf_op jit(solution)/shard_map/ppermute | solution.py:159
  29.9 19.5 %copy-start = (f32[32,64,128]{2,1,0:T(8,128)S(1)}, f32[32,64,128]{2,1,0:T(8,128)}, u32[]{:S(2)}) copy-start(f32[32,64,128]{2,1,0:T(8,128)} %get-tuple-element.17) | copy-start | bytes 3145732
  39.5 12.7 %collective-permute-start.6 = (f32[16,64,128]{2,1,0:T(8,128)S(1)}, f32[16,64,128]{2,1,0:T(8,128)}, u32[]{:S(2)}, u32[]{:S(2)}) collective-permute-start(f32[16,64,128]{2,1,0:T(8,128)S(1)} %slice_add_fusion), channel_id=1, source_target_pairs={{0,512},{16,528},{32,544},{48,560},{64,576},{80,592},{96,608},{112... | collective-permute-start | bytes 1572872 | tf_op jit(solution)/shard_map/ppermute | solution.py:168
  49.4 13.3 %collective-permute-start.3 = (f32[16,64,128]{2,1,0:T(8,128)S(1)}, f32[16,64,128]{2,1,0:T(8,128)}, u32[]{:S(2)}, u32[]{:S(2)}) collective-permute-start(f32[16,64,128]{2,1,0:T(8,128)S(1)} %slice_add_fusion.2), channel_id=1, source_target_pairs={{0,512},{16,528},{32,544},{48,560},{64,576},{80,592},{96,608},{112... | collective-permute-start | bytes 1572872 | tf_op jit(solution)/shard_map/ppermute | solution.py:168
  53.7 18.9 %collective-permute-start.7 = (f32[8,64,128]{2,1,0:T(8,128)S(1)}, f32[8,64,128]{2,1,0:T(8,128)}, u32[]{:S(2)}, u32[]{:S(2)}) collective-permute-start(f32[8,64,128]{2,1,0:T(8,128)S(1)} %constant_dynamic-slice_fusion), channel_id=1, source_target_pairs={{0,32},{1,481},{2,34},{3,483},{4,36},{5,485},{6,38},{7,487},{8,40}... | collective-permute-start | bytes 786440 | tf_op jit(solution)/shard_map/ppermute | solution.py:159
  63.9 14.6 %collective-permute-start.4 = (f32[8,64,128]{2,1,0:T(8,128)S(1)}, f32[8,64,128]{2,1,0:T(8,128)S(1)}, u32[]{:S(2)}, u32[]{:S(2)}) collective-permute-start(f32[8,64,128]{2,1,0:T(8,128)S(1)} %constant_dynamic-slice_fusion.1), channel_id=1, source_target_pairs={{0,32},{1,481},{2,34},{3,483},{4,36},{5,485},{6,38},{7,487},{8,40}... | collective-permute-start | bytes 786440 | tf_op jit(solution)/shard_map/ppermute | solution.py:159
  78.6 23.9 %collective-permute-start.8 = (f32[1,128,128]{2,1,0:T(8,128)S(1)}, f32[1,128,128]{2,1,0:T(8,128)S(1)}, u32[]{:S(2)}, u32[]{:S(2)}) collective-permute-start(f32[1,128,128]{2,1,0:T(8,128)S(1)} %get-tuple-element.31), channel_id=1, source_target_pairs={{0,64},{1,449},{2,66},{3,451},{4,68},{5,453},{6,70},{7,455},{8,72}... | collective-permute-start | bytes 196616 | tf_op jit(solution)/shard_map/ppermute | solution.py:159
  102.5 14.0 %collective-permute-start.10 = (f32[1,128,128]{2,1,0:T(8,128)S(1)}, f32[1,128,128]{2,1,0:T(8,128)S(1)}, u32[]{:S(2)}, u32[]{:S(2)}) collective-permute-start(f32[1,128,128]{2,1,0:T(8,128)S(1)} %get-tuple-element.21), channel_id=1, source_target_pairs={{0,448},{1,65},{2,450},{3,67},{4,452},{5,69},{6,454},{7,71},{8,456... | collective-permute-start | bytes 196616 | tf_op jit(solution)/shard_map/ppermute | solution.py:159
  110.4 10.1 %collective-permute-start.9 = (f32[1,128,128]{2,1,0:T(8,128)S(1)}, f32[1,128,128]{2,1,0:T(8,128)S(1)}, u32[]{:S(2)}, u32[]{:S(2)}) collective-permute-start(f32[1,128,128]{2,1,0:T(8,128)S(1)} %fusion.9), channel_id=1, source_target_pairs={{0,64},{1,449},{2,66},{3,451},{4,68},{5,453},{6,70},{7,455},{8,72}... | collective-permute-start | bytes 196616 | tf_op jit(solution)/shard_map/ppermute | solution.py:159
  120.5 10.1 %collective-permute-start.11 = (f32[1,128,128]{2,1,0:T(8,128)S(1)}, f32[1,128,128]{2,1,0:T(8,128)S(1)}, u32[]{:S(2)}, u32[]{:S(2)}) collective-permute-start(f32[1,128,128]{2,1,0:T(8,128)S(1)} %get-tuple-element.22), channel_id=1, source_target_pairs={{0,64},{1,449},{2,66},{3,451},{4,68},{5,453},{6,70},{7,455},{8,72}... | collective-permute-start | bytes 196616 | tf_op jit(solution)/shard_map/ppermute | solution.py:159
  122.5 10.7 %collective-permute-start.12 = (f32[1,128,128]{2,1,0:T(8,128)S(1)}, f32[1,128,128]{2,1,0:T(8,128)S(1)}, u32[]{:S(2)}, u32[]{:S(2)}) collective-permute-start(f32[1,128,128]{2,1,0:T(8,128)S(1)} %get-tuple-element.23), channel_id=1, source_target_pairs={{0,448},{1,65},{2,450},{3,67},{4,452},{5,69},{6,454},{7,71},{8,456... | collective-permute-start | bytes 196616 | tf_op jit(solution)/shard_map/ppermute | solution.py:159
  133.2 14.1 %collective-permute-start.13 = (f32[1,128,128]{2,1,0:T(8,128)S(1)}, f32[1,128,128]{2,1,0:T(8,128)S(1)}, u32[]{:S(2)}, u32[]{:S(2)}) collective-permute-start(f32[1,128,128]{2,1,0:T(8,128)S(1)} %get-tuple-element.24), channel_id=1, source_target_pairs={{0,64},{1,449},{2,66},{3,451},{4,68},{5,453},{6,70},{7,455},{8,72}... | collective-permute-start | bytes 196616 | tf_op jit(solution)/shard_map/ppermute | solution.py:159
  136.5 12.0 %collective-permute-start.14 = (f32[1,128,128]{2,1,0:T(8,128)S(1)}, f32[1,128,128]{2,1,0:T(8,128)S(1)}, u32[]{:S(2)}, u32[]{:S(2)}) collective-permute-start(f32[1,128,128]{2,1,0:T(8,128)S(1)} %get-tuple-element.25), channel_id=1, source_target_pairs={{0,448},{1,65},{2,450},{3,67},{4,452},{5,69},{6,454},{7,71},{8,456... | collective-permute-start | bytes 196616 | tf_op jit(solution)/shard_map/ppermute | solution.py:159
  144.0 10.6 %collective-permute-start.1 = (f32[3,128,128]{2,1,0:T(8,128)S(1)}, f32[3,128,128]{2,1,0:T(8,128)S(1)}, u32[]{:S(2)}, u32[]{:S(2)}) collective-permute-start(f32[3,128,128]{2,1,0:T(8,128)S(1)} %slice.52), channel_id=1, source_target_pairs={{0,8},{1,9},{2,10},{3,11},{4,12},{5,13},{6,14},{7,15},{8,0},{9,1},... | collective-permute-start | bytes 589832 | tf_op jit(solution)/shard_map/ppermute | solution.py:181
Sparse Core Ops, SparseCore 0:
  30.1 51.7 reduce-scatter.1

commit v3 on v2

--- a/solution.py
+++ b/solution.py
@@ -8,11 +8,11 @@
 from jax.sharding import PartitionSpec as P
 
 TILE = 128
-GROUP = 8
+GROUP = 16
 TILE_COPIES = 4
 ROWS = (64, 64)
 X_LO, X_HI, CORES = 2, 2, 2
-RING = 8
+RING = 4
 VMEM_LIMIT = 58 * 2**20
 
 root_two_pi = 0.7978845608028654
@@ -31,15 +31,21 @@
     return pl.ds(pl.multiple_of(index * TILE, TILE), TILE)
 
 
+def split(value, by):
+    quotient = (value * (-(-2**16 // by))) >> 16
+    return quotient, value - quotient * by
+
+
 def tile_place(owner, here, z_len):
-    other_x = (owner // z_len) ^ (here // z_len)
-    owner_z = owner % z_len
-    other_z = (owner_z ^ here) & 1
+    owner_x, owner_z = split(owner, z_len)
+    other_x, other_z = owner_x ^ split(here, z_len)[0], (owner_z ^ here) & 1
+    rest, _ = split(owner_z, 2)
     stride, chunk = 2, 0
     while z_len // stride > RING:
-        chunk = chunk * 2 + (owner_z // stride) % 2
+        rest, digit = split(rest, 2)
+        chunk = chunk * 2 + digit
         stride *= 2
-    return (other_z * 2 + other_x) * (z_len // 2) + chunk * RING + owner_z // stride
+    return (other_z * 2 + other_x) * (z_len // 2) + chunk * RING + rest
 
 
 def tile_copies(tiles_hbm, tiles_ref, sems):
@@ -54,7 +60,7 @@
     n_tiles, n_cols, per, z_len, y_len, slots_hbm, owners_hbm, x_hbm, g_hbm, tiles_hbm, send_hbm, keep_hbm, *refs
 ):
     outs, refs = refs[:2 * len(ROWS)], refs[2 * len(ROWS):]
-    x_ref, g_ref, tiles_ref, pre_ref, gp_ref, gi_ref, slots, owners, order, sems = refs
+    x_ref, g_ref, tiles_ref, pre_ref, gp_ref, gi_ref, slots, owners, order, row_of, col_of, sems = refs
     x_copy = pltpu.make_async_copy(x_hbm, x_ref, sems.at[TILE_COPIES])
     g_copy = pltpu.make_async_copy(g_hbm, g_ref, sems.at[TILE_COPIES + 1])
     scalars = [
@@ -70,20 +76,17 @@
     for copy in scalars:
         copy.wait()
 
-    def note(i, carry):
-        order[tile_place(owners[0, i], here, z_len)] = i
-        return carry
-
-    lax.fori_loop(0, n_tiles, note, 0)
     x_copy.wait()
 
     def project(step, carry):
         products = []
         for k in range(GROUP):
             i = step * GROUP + k
-            slot = slots[0, i]
-            products.append((slot % n_cols, jnp.dot(
-                x_ref[:, panel(slot // n_cols)], tiles_ref[i], preferred_element_type=jnp.float32
+            row, col = split(slots[0, i], n_cols)
+            order[tile_place(owners[0, i], here, z_len)] = i
+            row_of[i], col_of[i] = row, col
+            products.append((col, jnp.dot(
+                x_ref[:, panel(row)], tiles_ref[i], preferred_element_type=jnp.float32
             )))
         for col, product in products:
             pre_ref[col] += product
@@ -104,12 +107,12 @@
         products = []
         for k in range(GROUP):
             i = step * GROUP + k
-            row = slots[0, i] // n_cols
-            owner = row // per
-            core, y, x_hi = owner % CORES, (owner // CORES) % y_len, owner // (CORES * y_len)
-            core, x_hi = core ^ (near % CORES), x_hi ^ (near // (CORES * y_len))
-            products.append((((core * y_len + y) * X_HI + x_hi) * per + row % per, lax.dot_general(
-                gp_ref[slots[0, i] % n_cols], tiles_ref[i],
+            owner, spot = split(row_of[i], per)
+            owner, core = split(owner, CORES)
+            x_hi, y = split(owner, y_len)
+            spot = (((core ^ (near & 1)) * y_len + y) * X_HI + x_hi) * per + spot
+            products.append((spot, lax.dot_general(
+                gp_ref[col_of[i]], tiles_ref[i],
                 (((1,), (1,)), ((), ())), preferred_element_type=jnp.float32,
             )))
         for spot, product in products:
@@ -132,9 +135,9 @@
         def weight_grad(step, carry):
             for k in range(GROUP):
                 place = kind * n + step * GROUP + k
-                slot = slots[0, order[place]]
+                i = order[place]
                 product = lax.dot_general(
-                    x_ref[:, panel(slot // n_cols)], gp_ref[slot % n_cols],
+                    x_ref[:, panel(row_of[i])], gp_ref[col_of[i]],
                     (((0,), (0,)), ((), ())), preferred_element_type=jnp.float32,
                 )
                 start = 0
@@ -176,16 +179,13 @@
     return lax.ppermute(value, "tensor", [(i, i ^ 1) for i in range(sizes[1])])
 
 
-def swap_x_hi(value, sizes):
-    n_tensor = sizes[1]
-    return lax.ppermute(value, "tensor", [(i, (i + n_tensor // X_HI) % n_tensor) for i in range(n_tensor)])
-
-
-def sum_over_y(value, sizes):
+def sum_over(value, axis, sizes):
     y_len = sizes[1] // (X_HI * CORES)
-    groups = [
-        [(x * y_len + y) * CORES + c for y in range(y_len)] for x in range(X_HI) for c in range(CORES)
-    ]
+    index = lambda x, y, c: (x * y_len + y) * CORES + c
+    if axis == "y":
+        groups = [[index(x, y, c) for y in range(y_len)] for x in range(X_HI) for c in range(CORES)]
+    else:
+        groups = [[index(x, y, c) for x in range(X_HI)] for y in range(y_len) for c in range(CORES)]
     return lax.psum_scatter(value, "tensor", scatter_dimension=0, axis_index_groups=groups, tiled=True)
 
 
@@ -193,33 +193,36 @@
     z = lax.rem(lax.axis_index("dp"), sizes[0] // X_LO)
     core = lax.rem(lax.axis_index("tensor"), CORES)
     got_parts = [along_z(away, sizes, partner(1)) for away, _ in parts]
-    panels = sum_over_y(swap_cores(send, sizes) + keep, sizes)
+    panels = sum_over(swap_cores(send, sizes) + keep, "y", sizes)
     sums = []
     for got, (_, here) in zip(got_parts, parts):
         n = got.shape[0] // 2
-        now = got[:n] + here[:n] + swap_x(got[n:] + here[n:], sizes)
-        stride = 2
-        while now.shape[0] > RING:
-            half, digit = now.shape[0] // 2, lax.rem(lax.div(z, stride), 2)
-            now = pick(now, digit, half) + along_z(pick(now, 1 - digit, half), sizes, partner(stride))
-            stride *= 2
-        sums.append(now)
+        sums.append(got[:n] + here[:n] + swap_x(got[n:] + here[n:], sizes))
+    stride = 2
+    while sums[0].shape[0] > RING:
+        half, digit = sums[0].shape[0] // 2, lax.rem(lax.div(z, stride), 2)
+        if half == RING:
+            sums[-1], panels = lax.optimization_barrier((sums[-1], panels))
+            panels = sum_over(panels, "x_hi", sizes)
+        sums = [
+            pick(now, digit, half) + along_z(pick(now, 1 - digit, half), sizes, partner(stride)) for now in sums
+        ]
+        stride *= 2
     now = jnp.concatenate(sums, axis=1)
+    panels = jnp.concatenate([panels[j] for j in range(panels.shape[0])], axis=1)
     mine, way = lax.div(z, stride), 1 - 2 * core
     chunk = lambda k: pick(now, lax.rem(mine + k * way + RING, RING), 1)
     far, near, total = chunk(RING // 2), None, chunk(0)
     for k in range(RING // 2, 0, -1):
         if near is not None:
             far, near = lax.optimization_barrier((far, near))
+            near = along_z(near, sizes, lambda z, core: z - stride * (1 - 2 * core))
         far = along_z(far, sizes, lambda z, core: z + stride * (1 - 2 * core))
-        if near is not None:
-            near = along_z(near, sizes, lambda z, core: z - stride * (1 - 2 * core))
         if k > 1:
             far = far + chunk(k - 1)
             near = chunk(1 - k) if near is None else near + chunk(1 - k)
-    half = panels.shape[0] // 2
-    panels = swap_x_hi(panels[half:], sizes) + panels[:half]
-    return jnp.concatenate([panels[j] for j in range(half)], axis=1), total + far + near
+    far, near, panels = lax.optimization_barrier((far, near, panels))
+    return panels, total + far + near
 
 
 def on_device(n_dp, n_tensor, activations, grad_hidden, weight_tiles, tile_slots, owner_map):
@@ -249,7 +252,7 @@
             pltpu.VMEM((row_panels, tok_rows, TILE), jnp.float32),
             pltpu.SMEM((1, n_tiles), jnp.int32),
             pltpu.SMEM((1, n_tiles), jnp.int32),
-            pltpu.SMEM((n_tiles,), jnp.int32),
+            *[pltpu.SMEM((n_tiles,), jnp.int32)] * 3,
             pltpu.SemaphoreType.DMA((6 + TILE_COPIES,)),
         ],
         compiler_params=pltpu.CompilerParams(vmem_limit_bytes=VMEM_LIMIT),

time: 165 us -> 160 us (0.970)
  waiting for transfers between devices: 52.4 us -> 49.2 us
  Pallas kernels: 12.1 us -> 10.2 us
  other arithmetic: 10.1 us -> 8.37 us
    ppermute x2, waiting for transfers between devices: 0.01 us -> 5.97 us  [swap_x(): lax.ppermute(value, 'dp', [(i, (i + n_dp // X_LO) % n_dp) for i in range(...]
    ppermute x1 -> x0, waiting for transfers between devices: 5.48 us -> none  [swap_x_hi(): lax.ppermute(value, 'tensor', [(i, (i + n_tensor // X_HI) % n_tensor) for...]
    ppermute x11 -> x9, starting transfers between devices: 62.4 us -> 66.6 us  [along_z(): return lax.ppermute(value, ('dp', 'tensor'), pairs)]
    ppermute x11 -> x9, waiting for transfers between devices: 46.9 us -> 43.1 us  [along_z(): return lax.ppermute(value, ('dp', 'tensor'), pairs)]
    ppermute x1 -> x0, starting transfers between devices: 3.32 us -> none  [swap_x_hi(): lax.ppermute(value, 'tensor', [(i, (i + n_tensor // X_HI) % n_tensor) for...]
    pallas_call x1, Pallas kernels: 12.1 us -> 10.2 us  [on_device(): pl.pallas_call(functools.partial(tile_kernel, n_tiles, n_cols, per, z_len...]
    add x9 -> x6, other arithmetic: 8.33 us -> 7.55 us  [the longest x4 4.09 us: reduce_all(): sums.append(got[:n] + here[:n] + swap_x(got[n:] + here[n:], sizes))]
  transfers between devices with their start and end apart: 16 -> 14, of which waited for: 10 -> 6; matrix products, arithmetic and copies ran while one was open for 6% -> 6% of each run, Pallas kernels for 0% -> 0%
where the time goes in v3:
time: 160 us; the launch traced here: 158 us
  starting transfers between devices  74 us (46%)
  waiting for transfers between devices  49.2 us (31%)
  between operations  14.4 us (9%)
  Pallas kernels  10.2 us (6%)
  other arithmetic  8.37 us (5%)
  local copies, waits for them, and re-layouts  2.01 us (1%)
    ppermute x9, starting transfers between devices, along_z(): return lax.ppermute(value, ('dp', 'tensor'), pairs)  66.6 us
    ppermute x9, waiting for transfers between devices, along_z(): return lax.ppermute(value, ('dp', 'tensor'), pairs)  43.1 us
    pallas_call x1, Pallas kernels, on_device(): pl.pallas_call(functools.partial(tile_kernel, n_tiles, n_cols, per, z_len...  10.2 us
    ppermute x2, waiting for transfers between devices, swap_x(): lax.ppermute(value, 'dp', [(i, (i + n_dp // X_LO) % n_dp) for i in range(...  5.97 us
    ppermute x2, starting transfers between devices, swap_x(): lax.ppermute(value, 'dp', [(i, (i + n_dp // X_LO) % n_dp) for i in range(...  5.45 us
    add x4, other arithmetic, reduce_all(): sums.append(got[:n] + here[:n] + swap_x(got[n:] + here[n:], sizes))  4.09 us
  transfers between devices with their start and end apart: 14, of which 6 were waited for; matrix products, arithmetic and copies ran while one was open for 6% of the time, Pallas kernels for 0%

profile of v3, /device:TPU:6, one launch (start us, length us, event | category | flops | bytes accessed | tf_op | source)
XLA Modules:
  0.0 158.2 jit_solution(18346688786944724544)
XLA Ops:
  7.2 0.0 reduce-scatter.3.cloned.1.call-start
  7.2 10.2 %shard_map.68 = (f32[24,128,128]{2,1,0:T(8,128)}, f32[24,128,128]{2,1,0:T(8,128)}, f32[32,64,128]{2,1,0:T(8,128)}, f32[32,64,128]{2,1,0:T(8,128)}, f32[32,64,128]{2,1,0:T(8,128)}, /*index=5*/f32[32,64,128]{2,1,0:T(8,128)}) custom-call(s32[1,64]{1,0:T(1,128)} %slots_hbm.1, s32[1,64]{1,0:T(1,128)} %owners_hbm.1, bf16[128,6144]{1,0:T(8,128)(2,1)} %x_hbm.1, ...), custom_call_target="tpu_custom_call" | custom-call | flops 805306368 | bytes 12582912 | tf_op jit(solution)/shard_map/pallas_call | solution.py:241
  17.4 1.9 %collective-permute-start.7 = (f32[24,128,128]{2,1,0:T(8,128)}, f32[24,128,128]{2,1,0:T(8,128)S(1)}, u32[]{:S(2)}, u32[]{:S(2)}) collective-permute-start(f32[24,128,128]{2,1,0:T(8,128)} %get-tuple-element.19), channel_id=1, source_target_pairs={{0,1},{1,0},{2,3},{3,2},{4,5},{5,4},{6,7},{7,6},{8,9},{9,8},{10,11... | collective-permute-start | bytes 4718600 | tf_op jit(solution)/shard_map/ppermute | solution.py:179
  19.3 3.8 %collective-permute-start = (f32[32,64,128]{2,1,0:T(8,128)}, f32[32,64,128]{2,1,0:T(8,128)S(1)}, u32[]{:S(2)}, u32[]{:S(2)}) collective-permute-start(f32[32,64,128]{2,1,0:T(8,128)} %get-tuple-element.15), channel_id=1, source_target_pairs={{0,16},{1,497},{2,18},{3,499},{4,20},{5,501},{6,22},{7,503},{8,24}... | collective-permute-start | bytes 3145736 | tf_op jit(solution)/shard_map/ppermute | solution.py:162
  23.2 0.0 collective-permute-done.7
  23.2 2.8 %add.108 = f32[24,128,128]{2,1,0:T(8,128)} add(f32[24,128,128]{2,1,0:T(8,128)S(1)} %collective-permute-done.7, f32[24,128,128]{2,1,0:T(8,128)} %get-tuple-element.20) | non-fusion elementwise | flops 393216 | bytes 4718592 | tf_op jit(solution)/shard_map/add | solution.py:196
  26.0 0.0 copy-start.1
  26.0 0.0 copy-start
  26.0 0.0 reduce-scatter.3.cloned.1.call-update
  26.0 0.0 reduce-scatter.5.cloned.1.call-start
  26.1 3.7 %collective-permute-start.4 = (f32[32,64,128]{2,1,0:T(8,128)}, f32[32,64,128]{2,1,0:T(8,128)S(1)}, u32[]{:S(2)}, u32[]{:S(2)}) collective-permute-start(f32[32,64,128]{2,1,0:T(8,128)} %get-tuple-element.17), channel_id=1, source_target_pairs={{0,16},{1,497},{2,18},{3,499},{4,20},{5,501},{6,22},{7,503},{8,24}... | collective-permute-start | bytes 3145736 | tf_op jit(solution)/shard_map/ppermute | solution.py:162
  29.8 6.5 %collective-permute-done = f32[32,64,128]{2,1,0:T(8,128)S(1)} collective-permute-done((f32[32,64,128]{2,1,0:T(8,128)}, f32[32,64,128]{2,1,0:T(8,128)S(1)}, u32[]{:S(2)}, u32[]{:S(2)}) %collective-permute-start) | collective-permute-done | bytes 1048608 | tf_op jit(solution)/shard_map/ppermute | solution.py:162
  36.2 0.0 copy-done.1
  36.2 0.9 slice_add_fusion.2
  37.1 2.7 %collective-permute-start.1 = (f32[16,64,128]{2,1,0:T(8,128)}, f32[16,64,128]{2,1,0:T(8,128)}, u32[]{:S(2)}, u32[]{:S(2)}) collective-permute-start(f32[16,64,128]{2,1,0:T(8,128)} %slice_add_fusion.2), channel_id=1, source_target_pairs={{0,512},{16,528},{32,544},{48,560},{64,576},{80,592},{96,608},{112... | collective-permute-start | bytes 1572872 | tf_op jit(solution)/shard_map/ppermute | solution.py:171
  39.8 7.6 %collective-permute-done.4 = f32[32,64,128]{2,1,0:T(8,128)S(1)} collective-permute-done((f32[32,64,128]{2,1,0:T(8,128)}, f32[32,64,128]{2,1,0:T(8,128)S(1)}, u32[]{:S(2)}, u32[]{:S(2)}) %collective-permute-start.4) | collective-permute-done | bytes 1048608 | tf_op jit(solution)/shard_map/ppermute | solution.py:162
  47.5 0.0 copy-start.2
  47.5 1.0 copy-done.2
  48.5 0.0 copy-done
  48.5 0.9 slice_add_fusion
  49.3 2.7 %collective-permute-start.5 = (f32[16,64,128]{2,1,0:T(8,128)}, f32[16,64,128]{2,1,0:T(8,128)}, u32[]{:S(2)}, u32[]{:S(2)}) collective-permute-start(f32[16,64,128]{2,1,0:T(8,128)} %slice_add_fusion), channel_id=1, source_target_pairs={{0,512},{16,528},{32,544},{48,560},{64,576},{80,592},{96,608},{112... | collective-permute-start | bytes 1572872 | tf_op jit(solution)/shard_map/ppermute | solution.py:171
  52.1 0.0 copy-start.3
  52.1 0.0 collective-permute-done.1
  52.2 1.2 fusion.1
  53.4 5.7 %collective-permute-start.2 = (f32[8,64,128]{2,1,0:T(8,128)S(1)}, f32[8,64,128]{2,1,0:T(8,128)S(1)}, u32[]{:S(2)}, u32[]{:S(2)}) collective-permute-start(f32[8,64,128]{2,1,0:T(8,128)S(1)} %constant_dynamic-slice_fusion.3), channel_id=1, source_target_pairs={{0,32},{1,481},{2,34},{3,483},{4,36},{5,485},{6,38},{7,487},{8,40}... | collective-permute-start | bytes 786440 | tf_op jit(solution)/shard_map/ppermute | solution.py:162
  59.1 6.0 %collective-permute-done.5 = f32[16,64,128]{2,1,0:T(8,128)} collective-permute-done((f32[16,64,128]{2,1,0:T(8,128)}, f32[16,64,128]{2,1,0:T(8,128)}, u32[]{:S(2)}, u32[]{:S(2)}) %collective-permute-start.5) | collective-permute-done | bytes 524320 | tf_op jit(solution)/shard_map/ppermute | solution.py:171
  65.1 0.0 copy-done.3
  65.1 1.1 fusion
  66.3 5.2 %collective-permute-start.6 = (f32[8,64,128]{2,1,0:T(8,128)S(1)}, f32[8,64,128]{2,1,0:T(8,128)S(1)}, u32[]{:S(2)}, u32[]{:S(2)}) collective-permute-start(f32[8,64,128]{2,1,0:T(8,128)S(1)} %constant_dynamic-slice_fusion.1), channel_id=1, source_target_pairs={{0,32},{1,481},{2,34},{3,483},{4,36},{5,485},{6,38},{7,487},{8,40}... | collective-permute-start | bytes 786440 | tf_op jit(solution)/shard_map/ppermute | solution.py:162
  71.5 0.0 collective-permute-done.2
  71.6 9.1 %collective-permute-start.3 = (f32[4,64,128]{2,1,0:T(8,128)S(1)}, f32[4,64,128]{2,1,0:T(8,128)S(1)}, u32[]{:S(2)}, u32[]{:S(2)}) collective-permute-start(f32[4,64,128]{2,1,0:T(8,128)S(1)} %constant_dynamic-slice_fusion.2), channel_id=1, source_target_pairs={{0,64},{1,449},{2,66},{3,451},{4,68},{5,453},{6,70},{7,455},{8,72}... | collective-permute-start | bytes 393224 | tf_op jit(solution)/shard_map/ppermute | solution.py:162
  80.6 0.0 collective-permute-done.6
  80.7 0.0 reduce-scatter.3.cloned.1.call-done
  80.7 0.0 reduce-scatter.5.cloned.1.call-update
  80.8 6.3 %collective-permute-start.8 = (f32[4,64,128]{2,1,0:T(8,128)S(1)}, f32[4,64,128]{2,1,0:T(8,128)S(1)}, u32[]{:S(2)}, u32[]{:S(2)}) collective-permute-start(f32[4,64,128]{2,1,0:T(8,128)S(1)} %constant_dynamic-slice_fusion), channel_id=1, source_target_pairs={{0,64},{1,449},{2,66},{3,451},{4,68},{5,453},{6,70},{7,455},{8,72}... | collective-permute-start | bytes 393224 | tf_op jit(solution)/shard_map/ppermute | solution.py:162
  87.1 0.0 collective-permute-done.3
  87.1 7.0 %collective-permute-done.8 = f32[4,64,128]{2,1,0:T(8,128)S(1)} collective-permute-done((f32[4,64,128]{2,1,0:T(8,128)S(1)}, f32[4,64,128]{2,1,0:T(8,128)S(1)}, u32[]{:S(2)}, u32[]{:S(2)}) %collective-permute-start.8) | collective-permute-done | bytes 131104 | tf_op jit(solution)/shard_map/ppermute | solution.py:162
  94.1 13.9 %collective-permute-start.9 = (f32[1,128,128]{2,1,0:T(8,128)S(1)}, f32[1,128,128]{2,1,0:T(8,128)S(1)}, u32[]{:S(2)}, u32[]{:S(2)}) collective-permute-start(f32[1,128,128]{2,1,0:T(8,128)S(1)} %get-tuple-element.29), channel_id=1, source_target_pairs={{0,128},{1,385},{2,130},{3,387},{4,132},{5,389},{6,134},{7,391},{8... | collective-permute-start | bytes 196616 | tf_op jit(solution)/shard_map/ppermute | solution.py:162
  108.0 14.5 %collective-permute-done.9 = f32[1,128,128]{2,1,0:T(8,128)S(1)} collective-permute-done((f32[1,128,128]{2,1,0:T(8,128)S(1)}, f32[1,128,128]{2,1,0:T(8,128)S(1)}, u32[]{:S(2)}, u32[]{:S(2)}) %collective-permute-start.9) | collective-permute-done | bytes 65568 | tf_op jit(solution)/shard_map/ppermute | solution.py:162
  122.5 6.6 %collective-permute-start.10 = (f32[1,128,128]{2,1,0:T(8,128)S(1)}, f32[1,128,128]{2,1,0:T(8,128)S(1)}, u32[]{:S(2)}, u32[]{:S(2)}) collective-permute-start(f32[1,128,128]{2,1,0:T(8,128)S(1)} %fusion.7), channel_id=1, source_target_pairs={{0,128},{1,385},{2,130},{3,387},{4,132},{5,389},{6,134},{7,391},{8... | collective-permute-start | bytes 196616 | tf_op jit(solution)/shard_map/ppermute | solution.py:162
  129.2 12.3 %collective-permute-start.11 = (f32[1,128,128]{2,1,0:T(8,128)S(1)}, f32[1,128,128]{2,1,0:T(8,128)S(1)}, u32[]{:S(2)}, u32[]{:S(2)}) collective-permute-start(f32[1,128,128]{2,1,0:T(8,128)S(1)} %get-tuple-element.23), channel_id=1, source_target_pairs={{0,384},{1,129},{2,386},{3,131},{4,388},{5,133},{6,390},{7,135},{8... | collective-permute-start | bytes 196616 | tf_op jit(solution)/shard_map/ppermute | solution.py:162
  141.4 0.0 reduce-scatter.5.cloned.1.call-done
  141.5 0.9 slice_bitcast_fusion.2
  142.4 0.7 pad_maximum_fusion
  143.1 7.6 %collective-permute-done.10 = f32[1,128,128]{2,1,0:T(8,128)S(1)} collective-permute-done((f32[1,128,128]{2,1,0:T(8,128)S(1)}, f32[1,128,128]{2,1,0:T(8,128)S(1)}, u32[]{:S(2)}, u32[]{:S(2)}) %collective-permute-start.10) | collective-permute-done | bytes 65568 | tf_op jit(solution)/shard_map/ppermute | solution.py:162
  150.7 0.0 collective-permute-done.11
  150.7 0.6 fusion.4
  (10 shorter events, 0.2 us)
Async XLA Ops:
  7.2 73.5 %reduce-scatter.3.cloned.1.call-start = ((), (), s32[]{:S(2)}) async-start(), calls=%async_computation.2 | async-start | bytes 1966080 | tf_op jit(solution)/shard_map/reduce_scatter | solution.py:189
  17.4 5.8 %collective-permute-start.7 = (f32[24,128,128]{2,1,0:T(8,128)}, f32[24,128,128]{2,1,0:T(8,128)S(1)}, u32[]{:S(2)}, u32[]{:S(2)}) collective-permute-start(f32[24,128,128]{2,1,0:T(8,128)} %get-tuple-element.19), channel_id=1, source_target_pairs={{0,1},{1,0},{2,3},{3,2},{4,5},{5,4},{6,7},{7,6},{8,9},{9,8},{10,11... | collective-permute-start | bytes 4718600 | tf_op jit(solution)/shard_map/ppermute | solution.py:179
  19.3 16.9 %collective-permute-start = (f32[32,64,128]{2,1,0:T(8,128)}, f32[32,64,128]{2,1,0:T(8,128)S(1)}, u32[]{:S(2)}, u32[]{:S(2)}) collective-permute-start(f32[32,64,128]{2,1,0:T(8,128)} %get-tuple-element.15), channel_id=1, source_target_pairs={{0,16},{1,497},{2,18},{3,499},{4,20},{5,501},{6,22},{7,503},{8,24}... | collective-permute-start | bytes 3145736 | tf_op jit(solution)/shard_map/ppermute | solution.py:162
  26.0 10.3 %copy-start.1 = (f32[32,64,128]{2,1,0:T(8,128)S(1)}, f32[32,64,128]{2,1,0:T(8,128)}, u32[]{:S(2)}) copy-start(f32[32,64,128]{2,1,0:T(8,128)} %get-tuple-element.16) | copy-start | bytes 3145732
  26.0 22.5 %copy-start = (f32[32,64,128]{2,1,0:T(8,128)S(1)}, f32[32,64,128]{2,1,0:T(8,128)}, u32[]{:S(2)}) copy-start(f32[32,64,128]{2,1,0:T(8,128)} %get-tuple-element.18) | copy-start | bytes 3145732
  26.0 115.5 %reduce-scatter.5.cloned.1.call-start = ((), (), s32[]{:S(2)}) async-start(), calls=%async_computation.3 | async-start | bytes 589824 | tf_op jit(solution)/shard_map/reduce_scatter | solution.py:189
  26.1 21.4 %collective-permute-start.4 = (f32[32,64,128]{2,1,0:T(8,128)}, f32[32,64,128]{2,1,0:T(8,128)S(1)}, u32[]{:S(2)}, u32[]{:S(2)}) collective-permute-start(f32[32,64,128]{2,1,0:T(8,128)} %get-tuple-element.17), channel_id=1, source_target_pairs={{0,16},{1,497},{2,18},{3,499},{4,20},{5,501},{6,22},{7,503},{8,24}... | collective-permute-start | bytes 3145736 | tf_op jit(solution)/shard_map/ppermute | solution.py:162
  37.1 15.0 %collective-permute-start.1 = (f32[16,64,128]{2,1,0:T(8,128)}, f32[16,64,128]{2,1,0:T(8,128)}, u32[]{:S(2)}, u32[]{:S(2)}) collective-permute-start(f32[16,64,128]{2,1,0:T(8,128)} %slice_add_fusion.2), channel_id=1, source_target_pairs={{0,512},{16,528},{32,544},{48,560},{64,576},{80,592},{96,608},{112... | collective-permute-start | bytes 1572872 | tf_op jit(solution)/shard_map/ppermute | solution.py:171
  47.5 1.0 copy-start.2
  49.3 15.8 %collective-permute-start.5 = (f32[16,64,128]{2,1,0:T(8,128)}, f32[16,64,128]{2,1,0:T(8,128)}, u32[]{:S(2)}, u32[]{:S(2)}) collective-permute-start(f32[16,64,128]{2,1,0:T(8,128)} %slice_add_fusion), channel_id=1, source_target_pairs={{0,512},{16,528},{32,544},{48,560},{64,576},{80,592},{96,608},{112... | collective-permute-start | bytes 1572872 | tf_op jit(solution)/shard_map/ppermute | solution.py:171
  52.1 13.0 %copy-start.3 = (f32[32,64,128]{2,1,0:T(8,128)S(1)}, f32[32,64,128]{2,1,0:T(8,128)}, u32[]{:S(2)}) copy-start(f32[32,64,128]{2,1,0:T(8,128)} %copy-done.2) | copy-start | bytes 3145732
  53.4 18.1 %collective-permute-start.2 = (f32[8,64,128]{2,1,0:T(8,128)S(1)}, f32[8,64,128]{2,1,0:T(8,128)S(1)}, u32[]{:S(2)}, u32[]{:S(2)}) collective-permute-start(f32[8,64,128]{2,1,0:T(8,128)S(1)} %constant_dynamic-slice_fusion.3), channel_id=1, source_target_pairs={{0,32},{1,481},{2,34},{3,483},{4,36},{5,485},{6,38},{7,487},{8,40}... | collective-permute-start | bytes 786440 | tf_op jit(solution)/shard_map/ppermute | solution.py:162
  66.3 14.4 %collective-permute-start.6 = (f32[8,64,128]{2,1,0:T(8,128)S(1)}, f32[8,64,128]{2,1,0:T(8,128)S(1)}, u32[]{:S(2)}, u32[]{:S(2)}) collective-permute-start(f32[8,64,128]{2,1,0:T(8,128)S(1)} %constant_dynamic-slice_fusion.1), channel_id=1, source_target_pairs={{0,32},{1,481},{2,34},{3,483},{4,36},{5,485},{6,38},{7,487},{8,40}... | collective-permute-start | bytes 786440 | tf_op jit(solution)/shard_map/ppermute | solution.py:162
  71.6 15.5 %collective-permute-start.3 = (f32[4,64,128]{2,1,0:T(8,128)S(1)}, f32[4,64,128]{2,1,0:T(8,128)S(1)}, u32[]{:S(2)}, u32[]{:S(2)}) collective-permute-start(f32[4,64,128]{2,1,0:T(8,128)S(1)} %constant_dynamic-slice_fusion.2), channel_id=1, source_target_pairs={{0,64},{1,449},{2,66},{3,451},{4,68},{5,453},{6,70},{7,455},{8,72}... | collective-permute-start | bytes 393224 | tf_op jit(solution)/shard_map/ppermute | solution.py:162
  80.8 13.3 %collective-permute-start.8 = (f32[4,64,128]{2,1,0:T(8,128)S(1)}, f32[4,64,128]{2,1,0:T(8,128)S(1)}, u32[]{:S(2)}, u32[]{:S(2)}) collective-permute-start(f32[4,64,128]{2,1,0:T(8,128)S(1)} %constant_dynamic-slice_fusion), channel_id=1, source_target_pairs={{0,64},{1,449},{2,66},{3,451},{4,68},{5,453},{6,70},{7,455},{8,72}... | collective-permute-start | bytes 393224 | tf_op jit(solution)/shard_map/ppermute | solution.py:162
  94.1 28.4 %collective-permute-start.9 = (f32[1,128,128]{2,1,0:T(8,128)S(1)}, f32[1,128,128]{2,1,0:T(8,128)S(1)}, u32[]{:S(2)}, u32[]{:S(2)}) collective-permute-start(f32[1,128,128]{2,1,0:T(8,128)S(1)} %get-tuple-element.29), channel_id=1, source_target_pairs={{0,128},{1,385},{2,130},{3,387},{4,132},{5,389},{6,134},{7,391},{8... | collective-permute-start | bytes 196616 | tf_op jit(solution)/shard_map/ppermute | solution.py:162
  122.5 28.2 %collective-permute-start.10 = (f32[1,128,128]{2,1,0:T(8,128)S(1)}, f32[1,128,128]{2,1,0:T(8,128)S(1)}, u32[]{:S(2)}, u32[]{:S(2)}) collective-permute-start(f32[1,128,128]{2,1,0:T(8,128)S(1)} %fusion.7), channel_id=1, source_target_pairs={{0,128},{1,385},{2,130},{3,387},{4,132},{5,389},{6,134},{7,391},{8... | collective-permute-start | bytes 196616 | tf_op jit(solution)/shard_map/ppermute | solution.py:162
  129.2 21.5 %collective-permute-start.11 = (f32[1,128,128]{2,1,0:T(8,128)S(1)}, f32[1,128,128]{2,1,0:T(8,128)S(1)}, u32[]{:S(2)}, u32[]{:S(2)}) collective-permute-start(f32[1,128,128]{2,1,0:T(8,128)S(1)} %get-tuple-element.23), channel_id=1, source_target_pairs={{0,384},{1,129},{2,386},{3,131},{4,388},{5,133},{6,390},{7,135},{8... | collective-permute-start | bytes 196616 | tf_op jit(solution)/shard_map/ppermute | solution.py:162
Sparse Core Ops, SparseCore 0:
  26.1 50.7 reduce-scatter.2
  80.9 42.9 reduce-scatter.4

commit v4 on v3

--- a/solution.py
+++ b/solution.py
@@ -10,7 +10,9 @@
 TILE = 128
 GROUP = 16
 TILE_COPIES = 4
-ROWS = (64, 64)
+ROWS = (48, 32, 48)
+X_FIRST = (False, True, False)
+GROUPED = ((0, 1), (2,))
 X_LO, X_HI, CORES = 2, 2, 2
 RING = 4
 VMEM_LIMIT = 58 * 2**20
@@ -142,7 +144,8 @@
                 )
                 start = 0
                 for p, rows in enumerate(ROWS):
-                    outs[2 * p + other_z][other_x * n + step * GROUP + k] = product[start:start + rows]
+                    first, second = (other_x, other_z) if X_FIRST[p] else (other_z, other_x)
+                    outs[2 * p + first][second * n + step * GROUP + k] = product[start:start + rows]
                     start += rows
             return carry
 
@@ -192,12 +195,15 @@
 def reduce_all(parts, send, keep, sizes):
     z = lax.rem(lax.axis_index("dp"), sizes[0] // X_LO)
     core = lax.rem(lax.axis_index("tensor"), CORES)
-    got_parts = [along_z(away, sizes, partner(1)) for away, _ in parts]
+    pair_z = lambda value: along_z(value, sizes, partner(1))
+    pair_x = lambda value: swap_x(value, sizes)
+    got_parts = [(pair_x if x_first else pair_z)(away) for (away, _), x_first in zip(parts, X_FIRST)]
     panels = sum_over(swap_cores(send, sizes) + keep, "y", sizes)
     sums = []
-    for got, (_, here) in zip(got_parts, parts):
+    for got, (_, here), x_first in zip(got_parts, parts, X_FIRST):
         n = got.shape[0] // 2
-        sums.append(got[:n] + here[:n] + swap_x(got[n:] + here[n:], sizes))
+        sums.append(got[:n] + here[:n] + (pair_z if x_first else pair_x)(got[n:] + here[n:]))
+    sums = [jnp.concatenate([sums[p] for p in group], axis=1) for group in GROUPED]
     stride = 2
     while sums[0].shape[0] > RING:
         half, digit = sums[0].shape[0] // 2, lax.rem(lax.div(z, stride), 2)

time: 160 us -> 157 us (0.981)
  waiting for transfers between devices: 49.2 us -> 40.3 us
  starting transfers between devices: 74 us -> 82.3 us
  other arithmetic: 8.37 us -> 6.69 us
    ppermute x9 -> x10, waiting for transfers between devices: 43.1 us -> 27.4 us  [along_z(): return lax.ppermute(value, ('dp', 'tensor'), pairs)]
    ppermute x9 -> x10, starting transfers between devices: 66.6 us -> 71.8 us  [along_z(): return lax.ppermute(value, ('dp', 'tensor'), pairs)]
    ppermute x1, waiting for transfers between devices: 0.01 us -> 3.59 us  [swap_cores(): return lax.ppermute(value, 'tensor', [(i, i ^ 1) for i in range(sizes[1])])]
    ppermute x2 -> x3, waiting for transfers between devices: 5.97 us -> 9.24 us  [swap_x(): lax.ppermute(value, 'dp', [(i, (i + n_dp // X_LO) % n_dp) for i in range(...]
    ppermute x2 -> x3, starting transfers between devices: 5.45 us -> 8.58 us  [swap_x(): lax.ppermute(value, 'dp', [(i, (i + n_dp // X_LO) % n_dp) for i in range(...]
    add x4 -> x6, other arithmetic: 4.09 us -> 2.39 us  [the longest x3 1.21 us: reduce_all(): got[n:] + here[n:]]
  transfers between devices with their start and end apart: 14 -> 16, of which waited for: 6 -> 7; matrix products, arithmetic and copies ran while one was open for 6% -> 3% of each run, Pallas kernels for 0% -> 0%
where the time goes in v4:
time: 157 us; the launch traced here: 155 us
  starting transfers between devices  82.3 us (52%)
  waiting for transfers between devices  40.3 us (26%)
  between operations  14.5 us (9%)
  Pallas kernels  10.2 us (6%)
  other arithmetic  6.69 us (4%)
    ppermute x10, starting transfers between devices, along_z(): return lax.ppermute(value, ('dp', 'tensor'), pairs)  71.8 us
    ppermute x10, waiting for transfers between devices, along_z(): return lax.ppermute(value, ('dp', 'tensor'), pairs)  27.4 us
    pallas_call x1, Pallas kernels, on_device(): pl.pallas_call(functools.partial(tile_kernel, n_tiles, n_cols, per, z_len...  10.2 us
    ppermute x3, waiting for transfers between devices, swap_x(): lax.ppermute(value, 'dp', [(i, (i + n_dp // X_LO) % n_dp) for i in range(...  9.24 us
    ppermute x3, starting transfers between devices, swap_x(): lax.ppermute(value, 'dp', [(i, (i + n_dp // X_LO) % n_dp) for i in range(...  8.58 us
    ppermute x1, waiting for transfers between devices, swap_cores(): return lax.ppermute(value, 'tensor', [(i, i ^ 1) for i in range(sizes[1])])  3.59 us
  transfers between devices with their start and end apart: 16, of which 7 were waited for; matrix products, arithmetic and copies ran while one was open for 3% of the time, Pallas kernels for 0%

profile of v4, /device:TPU:6, one launch (start us, length us, event | category | flops | bytes accessed | tf_op | source)
XLA Modules:
  0.0 155.0 jit_solution(17609484118828440709)
XLA Ops:
  7.2 0.0 reduce-scatter.3.cloned.1.call-start
  7.2 10.2 %shard_map.68 = (f32[24,128,128]{2,1,0:T(8,128)}, f32[24,128,128]{2,1,0:T(8,128)}, f32[32,48,128]{2,1,0:T(8,128)}, f32[32,48,128]{2,1,0:T(8,128)}, f32[32,32,128...) custom-call(s32[1,64]{1,0:T(1,128)} %slots_hbm.1, s32[1,64]{1,0:T(1,128)} %owners_hbm.1, ...), custom_call_target="tpu_custom_call" | custom-call | flops 805306368 | bytes 12582912 | tf_op jit(solution)/shard_map/pallas_call | solution.py:247
  17.4 1.9 %collective-permute-start.9 = (f32[24,128,128]{2,1,0:T(8,128)}, f32[24,128,128]{2,1,0:T(8,128)S(1)}, u32[]{:S(2)}, u32[]{:S(2)}) collective-permute-start(f32[24,128,128]{2,1,0:T(8,128)} %get-tuple-element.23), channel_id=1, source_target_pairs={{0,1},{1,0},{2,3},{3,2},{4,5},{5,4},{6,7},{7,6},{8,9},{9,8},{10,11... | collective-permute-start | bytes 4718600 | tf_op jit(solution)/shard_map/ppermute | solution.py:182
  19.3 3.6 %collective-permute-done.9 = f32[24,128,128]{2,1,0:T(8,128)S(1)} collective-permute-done((f32[24,128,128]{2,1,0:T(8,128)}, f32[24,128,128]{2,1,0:T(8,128)S(1)}, u32[]{:S(2)}, u32[]{:S(2)}) %collective-permute-start.9) | collective-permute-done | bytes 1572896 | tf_op jit(solution)/shard_map/ppermute | solution.py:182
  22.9 2.8 %add.120 = f32[24,128,128]{2,1,0:T(8,128)} add(f32[24,128,128]{2,1,0:T(8,128)S(1)} %collective-permute-done.9, f32[24,128,128]{2,1,0:T(8,128)} %get-tuple-element.24) | non-fusion elementwise | flops 393216 | bytes 4718592 | tf_op jit(solution)/shard_map/add | solution.py:201
  25.7 0.0 copy-start.1
  25.7 0.0 copy-start
  25.7 0.0 reduce-scatter.3.cloned.1.call-update
  25.7 0.0 reduce-scatter.5.cloned.1.call-start
  25.8 4.0 %collective-permute-start = (f32[32,48,128]{2,1,0:T(8,128)}, f32[32,48,128]{2,1,0:T(8,128)S(1)}, u32[]{:S(2)}, u32[]{:S(2)}) collective-permute-start(f32[32,48,128]{2,1,0:T(8,128)} %get-tuple-element.17), channel_id=1, source_target_pairs={{0,16},{1,497},{2,18},{3,499},{4,20},{5,501},{6,22},{7,503},{8,24}... | collective-permute-start | bytes 2359304 | tf_op jit(solution)/shard_map/ppermute | solution.py:165
  29.8 2.7 %collective-permute-start.2 = (f32[32,32,128]{2,1,0:T(8,128)}, f32[32,32,128]{2,1,0:T(8,128)}, u32[]{:S(2)}, u32[]{:S(2)}) collective-permute-start(f32[32,32,128]{2,1,0:T(8,128)} %get-tuple-element.19), channel_id=1, source_target_pairs={{0,512},{16,528},{32,544},{48,560},{64,576},{80,592},{96,608},{112... | collective-permute-start | bytes 1572872 | tf_op jit(solution)/shard_map/ppermute | solution.py:174
  32.5 2.0 %collective-permute-start.6 = (f32[32,48,128]{2,1,0:T(8,128)}, f32[32,48,128]{2,1,0:T(8,128)S(1)}, u32[]{:S(2)}, u32[]{:S(2)}) collective-permute-start(f32[32,48,128]{2,1,0:T(8,128)} %get-tuple-element.21), channel_id=1, source_target_pairs={{0,16},{1,497},{2,18},{3,499},{4,20},{5,501},{6,22},{7,503},{8,24}... | collective-permute-start | bytes 2359304 | tf_op jit(solution)/shard_map/ppermute | solution.py:165
  34.6 6.5 %collective-permute-done.2 = f32[32,32,128]{2,1,0:T(8,128)} collective-permute-done((f32[32,32,128]{2,1,0:T(8,128)}, f32[32,32,128]{2,1,0:T(8,128)}, u32[]{:S(2)}, u32[]{:S(2)}) %collective-permute-start.2) | collective-permute-done | bytes 524320 | tf_op jit(solution)/shard_map/ppermute | solution.py:174
  41.2 1.1 slice_add_fusion.4
  42.3 7.0 %collective-permute-start.3 = (f32[16,32,128]{2,1,0:T(8,128)S(1)}, f32[16,32,128]{2,1,0:T(8,128)S(1)}, u32[]{:S(2)}, u32[]{:S(2)}) collective-permute-start(f32[16,32,128]{2,1,0:T(8,128)S(1)} %slice_add_fusion.4), channel_id=1, source_target_pairs={{0,16},{1,497},{2,18},{3,499},{4,20},{5,501},{6,22},{7,503},{8,24}... | collective-permute-start | bytes 786440 | tf_op jit(solution)/shard_map/ppermute | solution.py:165
  49.3 0.0 collective-permute-done
  49.3 0.0 copy-done.1
  49.3 2.7 %collective-permute-start.1 = (f32[16,48,128]{2,1,0:T(8,128)S(1)}, f32[16,48,128]{2,1,0:T(8,128)S(1)}, u32[]{:S(2)}, u32[]{:S(2)}) collective-permute-start(f32[16,48,128]{2,1,0:T(8,128)S(1)} %slice_add_fusion.2), channel_id=1, source_target_pairs={{0,512},{16,528},{32,544},{48,560},{64,576},{80,592},{96,608},{112... | collective-permute-start | bytes 1179656 | tf_op jit(solution)/shard_map/ppermute | solution.py:174
  52.1 0.0 collective-permute-done.6
  52.1 0.0 copy-done
  52.2 3.1 %collective-permute-start.7 = (f32[16,48,128]{2,1,0:T(8,128)S(1)}, f32[16,48,128]{2,1,0:T(8,128)S(1)}, u32[]{:S(2)}, u32[]{:S(2)}) collective-permute-start(f32[16,48,128]{2,1,0:T(8,128)S(1)} %slice_add_fusion), channel_id=1, source_target_pairs={{0,512},{16,528},{32,544},{48,560},{64,576},{80,592},{96,608},{112... | collective-permute-start | bytes 1179656 | tf_op jit(solution)/shard_map/ppermute | solution.py:174
  55.3 0.0 collective-permute-done.3
  55.3 0.0 copy-done.2
  55.3 1.0 fusion.5
  56.3 2.7 %collective-permute-done.1 = f32[16,48,128]{2,1,0:T(8,128)S(1)} collective-permute-done((f32[16,48,128]{2,1,0:T(8,128)S(1)}, f32[16,48,128]{2,1,0:T(8,128)S(1)}, u32[]{:S(2)}, u32[]{:S(2)}) %collective-permute-start.1) | collective-permute-done | bytes 393248 | tf_op jit(solution)/shard_map/ppermute | solution.py:174
  59.0 0.1 fusion.1
  59.1 8.1 %collective-permute-start.4 = (f32[8,80,128]{2,1,0:T(8,128)S(1)}, f32[8,80,128]{2,1,0:T(8,128)S(1)}, u32[]{:S(2)}, u32[]{:S(2)}) collective-permute-start(f32[8,80,128]{2,1,0:T(8,128)S(1)} %fusion.2), channel_id=1, source_target_pairs={{0,32},{1,481},{2,34},{3,483},{4,36},{5,485},{6,38},{7,487},{8,40}... | collective-permute-start | bytes 983048 | tf_op jit(solution)/shard_map/ppermute | solution.py:165
  67.2 0.0 collective-permute-done.7
  67.3 0.1 fusion
  67.4 7.2 %collective-permute-start.8 = (f32[8,48,128]{2,1,0:T(8,128)S(1)}, f32[8,48,128]{2,1,0:T(8,128)S(1)}, u32[]{:S(2)}, u32[]{:S(2)}) collective-permute-start(f32[8,48,128]{2,1,0:T(8,128)S(1)} %constant_dynamic-slice_fusion.1), channel_id=1, source_target_pairs={{0,32},{1,481},{2,34},{3,483},{4,36},{5,485},{6,38},{7,487},{8,40}... | collective-permute-start | bytes 589832 | tf_op jit(solution)/shard_map/ppermute | solution.py:165
  74.6 0.0 collective-permute-done.4
  74.7 11.4 %collective-permute-start.5 = (f32[4,80,128]{2,1,0:T(8,128)S(1)}, f32[4,80,128]{2,1,0:T(8,128)S(1)}, u32[]{:S(2)}, u32[]{:S(2)}) collective-permute-start(f32[4,80,128]{2,1,0:T(8,128)S(1)} %constant_dynamic-slice_fusion.2), channel_id=1, source_target_pairs={{0,64},{1,449},{2,66},{3,451},{4,68},{5,453},{6,70},{7,455},{8,72}... | collective-permute-start | bytes 491528 | tf_op jit(solution)/shard_map/ppermute | solution.py:165
  86.0 0.0 collective-permute-done.8
  86.1 0.0 reduce-scatter.3.cloned.1.call-done
  86.1 0.0 reduce-scatter.5.cloned.1.call-update
  86.2 2.9 %collective-permute-start.10 = (f32[4,48,128]{2,1,0:T(8,128)S(1)}, f32[4,48,128]{2,1,0:T(8,128)S(1)}, u32[]{:S(2)}, u32[]{:S(2)}) collective-permute-start(f32[4,48,128]{2,1,0:T(8,128)S(1)} %constant_dynamic-slice_fusion), channel_id=1, source_target_pairs={{0,64},{1,449},{2,66},{3,451},{4,68},{5,453},{6,70},{7,455},{8,72}... | collective-permute-start | bytes 294920 | tf_op jit(solution)/shard_map/ppermute | solution.py:165
  89.1 2.4 %collective-permute-done.5 = f32[4,80,128]{2,1,0:T(8,128)S(1)} collective-permute-done((f32[4,80,128]{2,1,0:T(8,128)S(1)}, f32[4,80,128]{2,1,0:T(8,128)S(1)}, u32[]{:S(2)}, u32[]{:S(2)}) %collective-permute-start.5) | collective-permute-done | bytes 163872 | tf_op jit(solution)/shard_map/ppermute | solution.py:165
  91.5 8.4 %collective-permute-done.10 = f32[4,48,128]{2,1,0:T(8,128)S(1)} collective-permute-done((f32[4,48,128]{2,1,0:T(8,128)S(1)}, f32[4,48,128]{2,1,0:T(8,128)S(1)}, u32[]{:S(2)}, u32[]{:S(2)}) %collective-permute-start.10) | collective-permute-done | bytes 98336 | tf_op jit(solution)/shard_map/ppermute | solution.py:165
  100.0 13.9 %collective-permute-start.11 = (f32[1,128,128]{2,1,0:T(8,128)S(1)}, f32[1,128,128]{2,1,0:T(8,128)S(1)}, u32[]{:S(2)}, u32[]{:S(2)}) collective-permute-start(f32[1,128,128]{2,1,0:T(8,128)S(1)} %get-tuple-element.33), channel_id=1, source_target_pairs={{0,128},{1,385},{2,130},{3,387},{4,132},{5,389},{6,134},{7,391},{8... | collective-permute-start | bytes 196616 | tf_op jit(solution)/shard_map/ppermute | solution.py:165
  113.9 5.2 %collective-permute-done.11 = f32[1,128,128]{2,1,0:T(8,128)S(1)} collective-permute-done((f32[1,128,128]{2,1,0:T(8,128)S(1)}, f32[1,128,128]{2,1,0:T(8,128)S(1)}, u32[]{:S(2)}, u32[]{:S(2)}) %collective-permute-start.11) | collective-permute-done | bytes 65568 | tf_op jit(solution)/shard_map/ppermute | solution.py:165
  119.1 13.0 %collective-permute-start.12 = (f32[1,128,128]{2,1,0:T(8,128)S(1)}, f32[1,128,128]{2,1,0:T(8,128)S(1)}, u32[]{:S(2)}, u32[]{:S(2)}) collective-permute-start(f32[1,128,128]{2,1,0:T(8,128)S(1)} %fusion.11), channel_id=1, source_target_pairs={{0,128},{1,385},{2,130},{3,387},{4,132},{5,389},{6,134},{7,391},{8... | collective-permute-start | bytes 196616 | tf_op jit(solution)/shard_map/ppermute | solution.py:165
  132.2 2.3 %collective-permute-start.13 = (f32[1,128,128]{2,1,0:T(8,128)S(1)}, f32[1,128,128]{2,1,0:T(8,128)S(1)}, u32[]{:S(2)}, u32[]{:S(2)}) collective-permute-start(f32[1,128,128]{2,1,0:T(8,128)S(1)} %get-tuple-element.27), channel_id=1, source_target_pairs={{0,384},{1,129},{2,386},{3,131},{4,388},{5,133},{6,390},{7,135},{8... | collective-permute-start | bytes 196616 | tf_op jit(solution)/shard_map/ppermute | solution.py:165
  134.5 0.0 reduce-scatter.5.cloned.1.call-done
  134.5 0.9 slice_bitcast_fusion.2
  135.4 0.7 pad_maximum_fusion
  136.1 0.0 collective-permute-done.12
  136.1 11.4 %collective-permute-done.13 = f32[1,128,128]{2,1,0:T(8,128)S(1)} collective-permute-done((f32[1,128,128]{2,1,0:T(8,128)S(1)}, f32[1,128,128]{2,1,0:T(8,128)S(1)}, u32[]{:S(2)}, u32[]{:S(2)}) %collective-permute-start.13) | collective-permute-done | bytes 65568 | tf_op jit(solution)/shard_map/ppermute | solution.py:165
  147.5 0.6 fusion.8
  (13 shorter events, 0.3 us)
Async XLA Ops:
  7.2 78.9 %reduce-scatter.3.cloned.1.call-start = ((), (), s32[]{:S(2)}) async-start(), calls=%async_computation.2 | async-start | bytes 1966080 | tf_op jit(solution)/shard_map/reduce_scatter | solution.py:192
  17.4 5.5 %collective-permute-start.9 = (f32[24,128,128]{2,1,0:T(8,128)}, f32[24,128,128]{2,1,0:T(8,128)S(1)}, u32[]{:S(2)}, u32[]{:S(2)}) collective-permute-start(f32[24,128,128]{2,1,0:T(8,128)} %get-tuple-element.23), channel_id=1, source_target_pairs={{0,1},{1,0},{2,3},{3,2},{4,5},{5,4},{6,7},{7,6},{8,9},{9,8},{10,11... | collective-permute-start | bytes 4718600 | tf_op jit(solution)/shard_map/ppermute | solution.py:182
  25.7 23.6 %copy-start.1 = (f32[32,48,128]{2,1,0:T(8,128)S(1)}, f32[32,48,128]{2,1,0:T(8,128)}, u32[]{:S(2)}) copy-start(f32[32,48,128]{2,1,0:T(8,128)} %get-tuple-element.18) | copy-start | bytes 2359300
  25.7 26.4 %copy-start = (f32[32,48,128]{2,1,0:T(8,128)S(1)}, f32[32,48,128]{2,1,0:T(8,128)}, u32[]{:S(2)}) copy-start(f32[32,48,128]{2,1,0:T(8,128)} %get-tuple-element.22) | copy-start | bytes 2359300
  25.7 108.7 %reduce-scatter.5.cloned.1.call-start = ((), (), s32[]{:S(2)}) async-start(), calls=%async_computation.3 | async-start | bytes 589824 | tf_op jit(solution)/shard_map/reduce_scatter | solution.py:192
  25.8 23.5 %collective-permute-start = (f32[32,48,128]{2,1,0:T(8,128)}, f32[32,48,128]{2,1,0:T(8,128)S(1)}, u32[]{:S(2)}, u32[]{:S(2)}) collective-permute-start(f32[32,48,128]{2,1,0:T(8,128)} %get-tuple-element.17), channel_id=1, source_target_pairs={{0,16},{1,497},{2,18},{3,499},{4,20},{5,501},{6,22},{7,503},{8,24}... | collective-permute-start | bytes 2359304 | tf_op jit(solution)/shard_map/ppermute | solution.py:165
  29.8 11.4 %collective-permute-start.2 = (f32[32,32,128]{2,1,0:T(8,128)}, f32[32,32,128]{2,1,0:T(8,128)}, u32[]{:S(2)}, u32[]{:S(2)}) collective-permute-start(f32[32,32,128]{2,1,0:T(8,128)} %get-tuple-element.19), channel_id=1, source_target_pairs={{0,512},{16,528},{32,544},{48,560},{64,576},{80,592},{96,608},{112... | collective-permute-start | bytes 1572872 | tf_op jit(solution)/shard_map/ppermute | solution.py:174
  32.5 19.6 %collective-permute-start.6 = (f32[32,48,128]{2,1,0:T(8,128)}, f32[32,48,128]{2,1,0:T(8,128)S(1)}, u32[]{:S(2)}, u32[]{:S(2)}) collective-permute-start(f32[32,48,128]{2,1,0:T(8,128)} %get-tuple-element.21), channel_id=1, source_target_pairs={{0,16},{1,497},{2,18},{3,499},{4,20},{5,501},{6,22},{7,503},{8,24}... | collective-permute-start | bytes 2359304 | tf_op jit(solution)/shard_map/ppermute | solution.py:165
  41.1 14.1 %copy-start.2 = (f32[32,32,128]{2,1,0:T(8,128)S(1)}, f32[32,32,128]{2,1,0:T(8,128)}, u32[]{:S(2)}) copy-start(f32[32,32,128]{2,1,0:T(8,128)} %get-tuple-element.20) | copy-start | bytes 1572868
  42.3 13.0 %collective-permute-start.3 = (f32[16,32,128]{2,1,0:T(8,128)S(1)}, f32[16,32,128]{2,1,0:T(8,128)S(1)}, u32[]{:S(2)}, u32[]{:S(2)}) collective-permute-start(f32[16,32,128]{2,1,0:T(8,128)S(1)} %slice_add_fusion.4), channel_id=1, source_target_pairs={{0,16},{1,497},{2,18},{3,499},{4,20},{5,501},{6,22},{7,503},{8,24}... | collective-permute-start | bytes 786440 | tf_op jit(solution)/shard_map/ppermute | solution.py:165
  49.3 9.7 %collective-permute-start.1 = (f32[16,48,128]{2,1,0:T(8,128)S(1)}, f32[16,48,128]{2,1,0:T(8,128)S(1)}, u32[]{:S(2)}, u32[]{:S(2)}) collective-permute-start(f32[16,48,128]{2,1,0:T(8,128)S(1)} %slice_add_fusion.2), channel_id=1, source_target_pairs={{0,512},{16,528},{32,544},{48,560},{64,576},{80,592},{96,608},{112... | collective-permute-start | bytes 1179656 | tf_op jit(solution)/shard_map/ppermute | solution.py:174
  52.2 15.1 %collective-permute-start.7 = (f32[16,48,128]{2,1,0:T(8,128)S(1)}, f32[16,48,128]{2,1,0:T(8,128)S(1)}, u32[]{:S(2)}, u32[]{:S(2)}) collective-permute-start(f32[16,48,128]{2,1,0:T(8,128)S(1)} %slice_add_fusion), channel_id=1, source_target_pairs={{0,512},{16,528},{32,544},{48,560},{64,576},{80,592},{96,608},{112... | collective-permute-start | bytes 1179656 | tf_op jit(solution)/shard_map/ppermute | solution.py:174
  59.1 15.4 %collective-permute-start.4 = (f32[8,80,128]{2,1,0:T(8,128)S(1)}, f32[8,80,128]{2,1,0:T(8,128)S(1)}, u32[]{:S(2)}, u32[]{:S(2)}) collective-permute-start(f32[8,80,128]{2,1,0:T(8,128)S(1)} %fusion.2), channel_id=1, source_target_pairs={{0,32},{1,481},{2,34},{3,483},{4,36},{5,485},{6,38},{7,487},{8,40}... | collective-permute-start | bytes 983048 | tf_op jit(solution)/shard_map/ppermute | solution.py:165
  67.4 18.7 %collective-permute-start.8 = (f32[8,48,128]{2,1,0:T(8,128)S(1)}, f32[8,48,128]{2,1,0:T(8,128)S(1)}, u32[]{:S(2)}, u32[]{:S(2)}) collective-permute-start(f32[8,48,128]{2,1,0:T(8,128)S(1)} %constant_dynamic-slice_fusion.1), channel_id=1, source_target_pairs={{0,32},{1,481},{2,34},{3,483},{4,36},{5,485},{6,38},{7,487},{8,40}... | collective-permute-start | bytes 589832 | tf_op jit(solution)/shard_map/ppermute | solution.py:165
  74.7 16.8 %collective-permute-start.5 = (f32[4,80,128]{2,1,0:T(8,128)S(1)}, f32[4,80,128]{2,1,0:T(8,128)S(1)}, u32[]{:S(2)}, u32[]{:S(2)}) collective-permute-start(f32[4,80,128]{2,1,0:T(8,128)S(1)} %constant_dynamic-slice_fusion.2), channel_id=1, source_target_pairs={{0,64},{1,449},{2,66},{3,451},{4,68},{5,453},{6,70},{7,455},{8,72}... | collective-permute-start | bytes 491528 | tf_op jit(solution)/shard_map/ppermute | solution.py:165
  86.2 13.8 %collective-permute-start.10 = (f32[4,48,128]{2,1,0:T(8,128)S(1)}, f32[4,48,128]{2,1,0:T(8,128)S(1)}, u32[]{:S(2)}, u32[]{:S(2)}) collective-permute-start(f32[4,48,128]{2,1,0:T(8,128)S(1)} %constant_dynamic-slice_fusion), channel_id=1, source_target_pairs={{0,64},{1,449},{2,66},{3,451},{4,68},{5,453},{6,70},{7,455},{8,72}... | collective-permute-start | bytes 294920 | tf_op jit(solution)/shard_map/ppermute | solution.py:165
  100.0 19.1 %collective-permute-start.11 = (f32[1,128,128]{2,1,0:T(8,128)S(1)}, f32[1,128,128]{2,1,0:T(8,128)S(1)}, u32[]{:S(2)}, u32[]{:S(2)}) collective-permute-start(f32[1,128,128]{2,1,0:T(8,128)S(1)} %get-tuple-element.33), channel_id=1, source_target_pairs={{0,128},{1,385},{2,130},{3,387},{4,132},{5,389},{6,134},{7,391},{8... | collective-permute-start | bytes 196616 | tf_op jit(solution)/shard_map/ppermute | solution.py:165
  119.1 17.0 %collective-permute-start.12 = (f32[1,128,128]{2,1,0:T(8,128)S(1)}, f32[1,128,128]{2,1,0:T(8,128)S(1)}, u32[]{:S(2)}, u32[]{:S(2)}) collective-permute-start(f32[1,128,128]{2,1,0:T(8,128)S(1)} %fusion.11), channel_id=1, source_target_pairs={{0,128},{1,385},{2,130},{3,387},{4,132},{5,389},{6,134},{7,391},{8... | collective-permute-start | bytes 196616 | tf_op jit(solution)/shard_map/ppermute | solution.py:165
  132.2 15.3 %collective-permute-start.13 = (f32[1,128,128]{2,1,0:T(8,128)S(1)}, f32[1,128,128]{2,1,0:T(8,128)S(1)}, u32[]{:S(2)}, u32[]{:S(2)}) collective-permute-start(f32[1,128,128]{2,1,0:T(8,128)S(1)} %get-tuple-element.27), channel_id=1, source_target_pairs={{0,384},{1,129},{2,386},{3,131},{4,388},{5,133},{6,390},{7,135},{8... | collective-permute-start | bytes 196616 | tf_op jit(solution)/shard_map/ppermute | solution.py:165
Sparse Core Ops, SparseCore 0:
  25.9 51.0 reduce-scatter.2
  86.3 37.6 reduce-scatter.4

commit v5 on v4

--- a/solution.py
+++ b/solution.py
@@ -218,12 +218,16 @@
     panels = jnp.concatenate([panels[j] for j in range(panels.shape[0])], axis=1)
     mine, way = lax.div(z, stride), 1 - 2 * core
     chunk = lambda k: pick(now, lax.rem(mine + k * way + RING, RING), 1)
-    far, near, total = chunk(RING // 2), None, chunk(0)
+    near, total = None, chunk(0)
+    far_way = lambda z, core: z + stride * (1 - 2 * core)
+    opposite = lax.rem(mine + RING // 2, RING)
+    far = jnp.concatenate([along_z(pick(part, opposite, 1), sizes, far_way) for part in sums], axis=1)
     for k in range(RING // 2, 0, -1):
         if near is not None:
             far, near = lax.optimization_barrier((far, near))
             near = along_z(near, sizes, lambda z, core: z - stride * (1 - 2 * core))
-        far = along_z(far, sizes, lambda z, core: z + stride * (1 - 2 * core))
+        if k < RING // 2:
+            far = along_z(far, sizes, far_way)
         if k > 1:
             far = far + chunk(k - 1)
             near = chunk(1 - k) if near is None else near + chunk(1 - k)

time: 157 us -> 167 us (1.064)
  starting transfers between devices: 82.3 us -> 102 us
  waiting for transfers between devices: 40.3 us -> 32.5 us
    ppermute x10 -> x11, starting transfers between devices: 71.8 us -> 91 us  [along_z(): return lax.ppermute(value, ('dp', 'tensor'), pairs)]
    ppermute x10 -> x11, waiting for transfers between devices: 27.4 us -> 19.6 us  [along_z(): return lax.ppermute(value, ('dp', 'tensor'), pairs)]
  transfers between devices with their start and end apart: 16 -> 17, of which waited for: 7 -> 6; matrix products, arithmetic and copies ran while one was open for 3% -> 3% of each run, Pallas kernels for 0% -> 0%
where the time goes in v5:
time: 167 us; the launch traced here: 166 us
  starting transfers between devices  102 us (61%)
  waiting for transfers between devices  32.5 us (19%)
  between operations  14.5 us (9%)
  Pallas kernels  10.2 us (6%)
  other arithmetic  6.68 us (4%)
    ppermute x11, starting transfers between devices, along_z(): return lax.ppermute(value, ('dp', 'tensor'), pairs)  91 us
    ppermute x11, waiting for transfers between devices, along_z(): return lax.ppermute(value, ('dp', 'tensor'), pairs)  19.6 us
    pallas_call x1, Pallas kernels, on_device(): pl.pallas_call(functools.partial(tile_kernel, n_tiles, n_cols, per, z_len...  10.2 us
    ppermute x3, waiting for transfers between devices, swap_x(): lax.ppermute(value, 'dp', [(i, (i + n_dp // X_LO) % n_dp) for i in range(...  9.26 us
    ppermute x3, starting transfers between devices, swap_x(): lax.ppermute(value, 'dp', [(i, (i + n_dp // X_LO) % n_dp) for i in range(...  8.58 us
    ppermute x1, waiting for transfers between devices, swap_cores(): return lax.ppermute(value, 'tensor', [(i, i ^ 1) for i in range(sizes[1])])  3.59 us
  transfers between devices with their start and end apart: 17, of which 6 were waited for; matrix products, arithmetic and copies ran while one was open for 3% of the time, Pallas kernels for 0%

profile of v5, /device:TPU:6, one launch (start us, length us, event | category | flops | bytes accessed | tf_op | source)
XLA Modules:
  0.0 166.4 jit_solution(13170091907463633584)
XLA Ops:
  7.2 0.0 reduce-scatter.3.cloned.1.call-start
  7.2 10.2 %shard_map.68 = (f32[24,128,128]{2,1,0:T(8,128)}, f32[24,128,128]{2,1,0:T(8,128)}, f32[32,48,128]{2,1,0:T(8,128)}, f32[32,48,128]{2,1,0:T(8,128)}, f32[32,32,128...) custom-call(s32[1,64]{1,0:T(1,128)} %slots_hbm.1, s32[1,64]{1,0:T(1,128)} %owners_hbm.1, ...), custom_call_target="tpu_custom_call" | custom-call | flops 805306368 | bytes 12582912 | tf_op jit(solution)/shard_map/pallas_call | solution.py:251
  17.4 1.9 %collective-permute-start.10 = (f32[24,128,128]{2,1,0:T(8,128)}, f32[24,128,128]{2,1,0:T(8,128)S(1)}, u32[]{:S(2)}, u32[]{:S(2)}) collective-permute-start(f32[24,128,128]{2,1,0:T(8,128)} %get-tuple-element.23), channel_id=1, source_target_pairs={{0,1},{1,0},{2,3},{3,2},{4,5},{5,4},{6,7},{7,6},{8,9},{9,8},{10,11... | collective-permute-start | bytes 4718600 | tf_op jit(solution)/shard_map/ppermute | solution.py:182
  19.3 3.6 %collective-permute-done.10 = f32[24,128,128]{2,1,0:T(8,128)S(1)} collective-permute-done((f32[24,128,128]{2,1,0:T(8,128)}, f32[24,128,128]{2,1,0:T(8,128)S(1)}, u32[]{:S(2)}, u32[]{:S(2)}) %collective-permute-start.10) | collective-permute-done | bytes 1572896 | tf_op jit(solution)/shard_map/ppermute | solution.py:182
  22.9 2.8 %add.120 = f32[24,128,128]{2,1,0:T(8,128)} add(f32[24,128,128]{2,1,0:T(8,128)S(1)} %collective-permute-done.10, f32[24,128,128]{2,1,0:T(8,128)} %get-tuple-element.24) | non-fusion elementwise | flops 393216 | bytes 4718592 | tf_op jit(solution)/shard_map/add | solution.py:201
  25.7 0.0 reduce-scatter.3.cloned.1.call-update
  25.8 0.0 reduce-scatter.5.cloned.1.call-start
  25.8 4.0 %collective-permute-start = (f32[32,48,128]{2,1,0:T(8,128)}, f32[32,48,128]{2,1,0:T(8,128)S(1)}, u32[]{:S(2)}, u32[]{:S(2)}) collective-permute-start(f32[32,48,128]{2,1,0:T(8,128)} %get-tuple-element.17), channel_id=1, source_target_pairs={{0,16},{1,497},{2,18},{3,499},{4,20},{5,501},{6,22},{7,503},{8,24}... | collective-permute-start | bytes 2359304 | tf_op jit(solution)/shard_map/ppermute | solution.py:165
  29.8 2.7 %collective-permute-start.2 = (f32[32,32,128]{2,1,0:T(8,128)}, f32[32,32,128]{2,1,0:T(8,128)}, u32[]{:S(2)}, u32[]{:S(2)}) collective-permute-start(f32[32,32,128]{2,1,0:T(8,128)} %get-tuple-element.19), channel_id=1, source_target_pairs={{0,512},{16,528},{32,544},{48,560},{64,576},{80,592},{96,608},{112... | collective-permute-start | bytes 1572872 | tf_op jit(solution)/shard_map/ppermute | solution.py:174
  32.5 2.0 %collective-permute-start.7 = (f32[32,48,128]{2,1,0:T(8,128)}, f32[32,48,128]{2,1,0:T(8,128)S(1)}, u32[]{:S(2)}, u32[]{:S(2)}) collective-permute-start(f32[32,48,128]{2,1,0:T(8,128)} %get-tuple-element.21), channel_id=1, source_target_pairs={{0,16},{1,497},{2,18},{3,499},{4,20},{5,501},{6,22},{7,503},{8,24}... | collective-permute-start | bytes 2359304 | tf_op jit(solution)/shard_map/ppermute | solution.py:165
  34.6 6.6 %collective-permute-done.2 = f32[32,32,128]{2,1,0:T(8,128)} collective-permute-done((f32[32,32,128]{2,1,0:T(8,128)}, f32[32,32,128]{2,1,0:T(8,128)}, u32[]{:S(2)}, u32[]{:S(2)}) %collective-permute-start.2) | collective-permute-done | bytes 524320 | tf_op jit(solution)/shard_map/ppermute | solution.py:174
  41.2 1.1 slice_add_fusion.4
  42.3 7.0 %collective-permute-start.3 = (f32[16,32,128]{2,1,0:T(8,128)S(1)}, f32[16,32,128]{2,1,0:T(8,128)S(1)}, u32[]{:S(2)}, u32[]{:S(2)}) collective-permute-start(f32[16,32,128]{2,1,0:T(8,128)S(1)} %slice_add_fusion.4), channel_id=1, source_target_pairs={{0,16},{1,497},{2,18},{3,499},{4,20},{5,501},{6,22},{7,503},{8,24}... | collective-permute-start | bytes 786440 | tf_op jit(solution)/shard_map/ppermute | solution.py:165
  49.3 0.0 collective-permute-done
  49.3 0.0 copy-done.1
  49.3 2.7 %collective-permute-start.1 = (f32[16,48,128]{2,1,0:T(8,128)S(1)}, f32[16,48,128]{2,1,0:T(8,128)S(1)}, u32[]{:S(2)}, u32[]{:S(2)}) collective-permute-start(f32[16,48,128]{2,1,0:T(8,128)S(1)} %slice_add_fusion.2), channel_id=1, source_target_pairs={{0,512},{16,528},{32,544},{48,560},{64,576},{80,592},{96,608},{112... | collective-permute-start | bytes 1179656 | tf_op jit(solution)/shard_map/ppermute | solution.py:174
  52.1 0.0 collective-permute-done.7
  52.1 0.0 copy-done
  52.2 3.1 %collective-permute-start.8 = (f32[16,48,128]{2,1,0:T(8,128)S(1)}, f32[16,48,128]{2,1,0:T(8,128)S(1)}, u32[]{:S(2)}, u32[]{:S(2)}) collective-permute-start(f32[16,48,128]{2,1,0:T(8,128)S(1)} %slice_add_fusion), channel_id=1, source_target_pairs={{0,512},{16,528},{32,544},{48,560},{64,576},{80,592},{96,608},{112... | collective-permute-start | bytes 1179656 | tf_op jit(solution)/shard_map/ppermute | solution.py:174
  55.3 0.0 collective-permute-done.3
  55.3 0.0 copy-done.2
  55.3 1.0 fusion.5
  56.3 2.7 %collective-permute-done.1 = f32[16,48,128]{2,1,0:T(8,128)S(1)} collective-permute-done((f32[16,48,128]{2,1,0:T(8,128)S(1)}, f32[16,48,128]{2,1,0:T(8,128)S(1)}, u32[]{:S(2)}, u32[]{:S(2)}) %collective-permute-start.1) | collective-permute-done | bytes 393248 | tf_op jit(solution)/shard_map/ppermute | solution.py:174
  59.0 0.1 fusion.1
  59.1 8.1 %collective-permute-start.4 = (f32[8,80,128]{2,1,0:T(8,128)S(1)}, f32[8,80,128]{2,1,0:T(8,128)S(1)}, u32[]{:S(2)}, u32[]{:S(2)}) collective-permute-start(f32[8,80,128]{2,1,0:T(8,128)S(1)} %fusion.2), channel_id=1, source_target_pairs={{0,32},{1,481},{2,34},{3,483},{4,36},{5,485},{6,38},{7,487},{8,40}... | collective-permute-start | bytes 983048 | tf_op jit(solution)/shard_map/ppermute | solution.py:165
  67.2 0.0 collective-permute-done.8
  67.2 0.1 fusion
  67.4 7.2 %collective-permute-start.9 = (f32[8,48,128]{2,1,0:T(8,128)S(1)}, f32[8,48,128]{2,1,0:T(8,128)S(1)}, u32[]{:S(2)}, u32[]{:S(2)}) collective-permute-start(f32[8,48,128]{2,1,0:T(8,128)S(1)} %constant_dynamic-slice_fusion.2), channel_id=1, source_target_pairs={{0,32},{1,481},{2,34},{3,483},{4,36},{5,485},{6,38},{7,487},{8,40}... | collective-permute-start | bytes 589832 | tf_op jit(solution)/shard_map/ppermute | solution.py:165
  74.6 0.0 collective-permute-done.4
  74.7 11.4 %collective-permute-start.5 = (f32[4,80,128]{2,1,0:T(8,128)S(1)}, f32[4,80,128]{2,1,0:T(8,128)S(1)}, u32[]{:S(2)}, u32[]{:S(2)}) collective-permute-start(f32[4,80,128]{2,1,0:T(8,128)S(1)} %constant_dynamic-slice_fusion.4), channel_id=1, source_target_pairs={{0,64},{1,449},{2,66},{3,451},{4,68},{5,453},{6,70},{7,455},{8,72}... | collective-permute-start | bytes 491528 | tf_op jit(solution)/shard_map/ppermute | solution.py:165
  86.0 0.0 collective-permute-done.9
  86.1 0.0 reduce-scatter.3.cloned.1.call-done
  86.1 0.0 reduce-scatter.5.cloned.1.call-update
  86.1 5.3 %collective-permute-done.5 = f32[4,80,128]{2,1,0:T(8,128)S(1)} collective-permute-done((f32[4,80,128]{2,1,0:T(8,128)S(1)}, f32[4,80,128]{2,1,0:T(8,128)S(1)}, u32[]{:S(2)}, u32[]{:S(2)}) %collective-permute-start.5) | collective-permute-done | bytes 163872 | tf_op jit(solution)/shard_map/ppermute | solution.py:165
  91.5 6.1 %collective-permute-start.11 = (f32[4,48,128]{2,1,0:T(8,128)S(1)}, f32[4,48,128]{2,1,0:T(8,128)S(1)}, u32[]{:S(2)}, u32[]{:S(2)}) collective-permute-start(f32[4,48,128]{2,1,0:T(8,128)S(1)} %constant_dynamic-slice_fusion.1), channel_id=1, source_target_pairs={{0,64},{1,449},{2,66},{3,451},{4,68},{5,453},{6,70},{7,455},{8,72}... | collective-permute-start | bytes 294920 | tf_op jit(solution)/shard_map/ppermute | solution.py:165
  97.6 16.7 %collective-permute-start.6 = (f32[1,80,128]{2,1,0:T(8,128)S(1)}, f32[1,80,128]{2,1,0:T(8,128)S(1)}, u32[]{:S(2)}, u32[]{:S(2)}) collective-permute-start(f32[1,80,128]{2,1,0:T(8,128)S(1)} %constant_dynamic-slice_fusion.3), channel_id=1, source_target_pairs={{0,128},{1,385},{2,130},{3,387},{4,132},{5,389},{6,134},{7,391},{8... | collective-permute-start | bytes 122888 | tf_op jit(solution)/shard_map/ppermute | solution.py:165
  114.3 0.0 collective-permute-done.11
  114.4 13.7 %collective-permute-start.12 = (f32[1,48,128]{2,1,0:T(8,128)S(1)}, f32[1,48,128]{2,1,0:T(8,128)S(1)}, u32[]{:S(2)}, u32[]{:S(2)}) collective-permute-start(f32[1,48,128]{2,1,0:T(8,128)S(1)} %constant_dynamic-slice_fusion), channel_id=1, source_target_pairs={{0,128},{1,385},{2,130},{3,387},{4,132},{5,389},{6,134},{7,391},{8... | collective-permute-start | bytes 73736 | tf_op jit(solution)/shard_map/ppermute | solution.py:165
  128.2 0.0 collective-permute-done.6
  128.2 1.4 collective-permute-done.12
  129.6 13.0 %collective-permute-start.13 = (f32[1,128,128]{2,1,0:T(8,128)S(1)}, f32[1,128,128]{2,1,0:T(8,128)S(1)}, u32[]{:S(2)}, u32[]{:S(2)}) collective-permute-start(f32[1,128,128]{2,1,0:T(8,128)S(1)} %get-tuple-element.26), channel_id=1, source_target_pairs={{0,128},{1,385},{2,130},{3,387},{4,132},{5,389},{6,134},{7,391},{8... | collective-permute-start | bytes 196616 | tf_op jit(solution)/shard_map/ppermute | solution.py:165
  142.6 1.9 %collective-permute-start.14 = (f32[1,128,128]{2,1,0:T(8,128)S(1)}, f32[1,128,128]{2,1,0:T(8,128)S(1)}, u32[]{:S(2)}, u32[]{:S(2)}) collective-permute-start(f32[1,128,128]{2,1,0:T(8,128)S(1)} %get-tuple-element.27), channel_id=1, source_target_pairs={{0,384},{1,129},{2,386},{3,131},{4,388},{5,133},{6,390},{7,135},{8... | collective-permute-start | bytes 196616 | tf_op jit(solution)/shard_map/ppermute | solution.py:165
  144.5 0.0 reduce-scatter.5.cloned.1.call-done
  144.5 0.9 slice_bitcast_fusion.2
  145.5 0.7 pad_maximum_fusion
  146.2 0.0 collective-permute-done.13
  146.2 12.8 %collective-permute-done.14 = f32[1,128,128]{2,1,0:T(8,128)S(1)} collective-permute-done((f32[1,128,128]{2,1,0:T(8,128)S(1)}, f32[1,128,128]{2,1,0:T(8,128)S(1)}, u32[]{:S(2)}, u32[]{:S(2)}) %collective-permute-start.14) | collective-permute-done | bytes 65568 | tf_op jit(solution)/shard_map/ppermute | solution.py:165
  158.9 0.6 fusion.8
  (16 shorter events, 0.3 us)
Async XLA Ops:
  7.2 78.9 %reduce-scatter.3.cloned.1.call-start = ((), (), s32[]{:S(2)}) async-start(), calls=%async_computation.2 | async-start | bytes 1966080 | tf_op jit(solution)/shard_map/reduce_scatter | solution.py:192
  17.4 5.5 %collective-permute-start.10 = (f32[24,128,128]{2,1,0:T(8,128)}, f32[24,128,128]{2,1,0:T(8,128)S(1)}, u32[]{:S(2)}, u32[]{:S(2)}) collective-permute-start(f32[24,128,128]{2,1,0:T(8,128)} %get-tuple-element.23), channel_id=1, source_target_pairs={{0,1},{1,0},{2,3},{3,2},{4,5},{5,4},{6,7},{7,6},{8,9},{9,8},{10,11... | collective-permute-start | bytes 4718600 | tf_op jit(solution)/shard_map/ppermute | solution.py:182
  25.7 23.6 %copy-start.1 = (f32[32,48,128]{2,1,0:T(8,128)S(1)}, f32[32,48,128]{2,1,0:T(8,128)}, u32[]{:S(2)}) copy-start(f32[32,48,128]{2,1,0:T(8,128)} %get-tuple-element.18) | copy-start | bytes 2359300
  25.7 26.4 %copy-start = (f32[32,48,128]{2,1,0:T(8,128)S(1)}, f32[32,48,128]{2,1,0:T(8,128)}, u32[]{:S(2)}) copy-start(f32[32,48,128]{2,1,0:T(8,128)} %get-tuple-element.22) | copy-start | bytes 2359300
  25.8 118.8 %reduce-scatter.5.cloned.1.call-start = ((), (), s32[]{:S(2)}) async-start(), calls=%async_computation.3 | async-start | bytes 589824 | tf_op jit(solution)/shard_map/reduce_scatter | solution.py:192
  25.8 23.5 %collective-permute-start = (f32[32,48,128]{2,1,0:T(8,128)}, f32[32,48,128]{2,1,0:T(8,128)S(1)}, u32[]{:S(2)}, u32[]{:S(2)}) collective-permute-start(f32[32,48,128]{2,1,0:T(8,128)} %get-tuple-element.17), channel_id=1, source_target_pairs={{0,16},{1,497},{2,18},{3,499},{4,20},{5,501},{6,22},{7,503},{8,24}... | collective-permute-start | bytes 2359304 | tf_op jit(solution)/shard_map/ppermute | solution.py:165
  29.8 11.4 %collective-permute-start.2 = (f32[32,32,128]{2,1,0:T(8,128)}, f32[32,32,128]{2,1,0:T(8,128)}, u32[]{:S(2)}, u32[]{:S(2)}) collective-permute-start(f32[32,32,128]{2,1,0:T(8,128)} %get-tuple-element.19), channel_id=1, source_target_pairs={{0,512},{16,528},{32,544},{48,560},{64,576},{80,592},{96,608},{112... | collective-permute-start | bytes 1572872 | tf_op jit(solution)/shard_map/ppermute | solution.py:174
  32.5 19.6 %collective-permute-start.7 = (f32[32,48,128]{2,1,0:T(8,128)}, f32[32,48,128]{2,1,0:T(8,128)S(1)}, u32[]{:S(2)}, u32[]{:S(2)}) collective-permute-start(f32[32,48,128]{2,1,0:T(8,128)} %get-tuple-element.21), channel_id=1, source_target_pairs={{0,16},{1,497},{2,18},{3,499},{4,20},{5,501},{6,22},{7,503},{8,24}... | collective-permute-start | bytes 2359304 | tf_op jit(solution)/shard_map/ppermute | solution.py:165
  41.2 14.1 %copy-start.2 = (f32[32,32,128]{2,1,0:T(8,128)S(1)}, f32[32,32,128]{2,1,0:T(8,128)}, u32[]{:S(2)}) copy-start(f32[32,32,128]{2,1,0:T(8,128)} %get-tuple-element.20) | copy-start | bytes 1572868
  42.3 13.0 %collective-permute-start.3 = (f32[16,32,128]{2,1,0:T(8,128)S(1)}, f32[16,32,128]{2,1,0:T(8,128)S(1)}, u32[]{:S(2)}, u32[]{:S(2)}) collective-permute-start(f32[16,32,128]{2,1,0:T(8,128)S(1)} %slice_add_fusion.4), channel_id=1, source_target_pairs={{0,16},{1,497},{2,18},{3,499},{4,20},{5,501},{6,22},{7,503},{8,24}... | collective-permute-start | bytes 786440 | tf_op jit(solution)/shard_map/ppermute | solution.py:165
  49.3 9.7 %collective-permute-start.1 = (f32[16,48,128]{2,1,0:T(8,128)S(1)}, f32[16,48,128]{2,1,0:T(8,128)S(1)}, u32[]{:S(2)}, u32[]{:S(2)}) collective-permute-start(f32[16,48,128]{2,1,0:T(8,128)S(1)} %slice_add_fusion.2), channel_id=1, source_target_pairs={{0,512},{16,528},{32,544},{48,560},{64,576},{80,592},{96,608},{112... | collective-permute-start | bytes 1179656 | tf_op jit(solution)/shard_map/ppermute | solution.py:174
  52.2 15.1 %collective-permute-start.8 = (f32[16,48,128]{2,1,0:T(8,128)S(1)}, f32[16,48,128]{2,1,0:T(8,128)S(1)}, u32[]{:S(2)}, u32[]{:S(2)}) collective-permute-start(f32[16,48,128]{2,1,0:T(8,128)S(1)} %slice_add_fusion), channel_id=1, source_target_pairs={{0,512},{16,528},{32,544},{48,560},{64,576},{80,592},{96,608},{112... | collective-permute-start | bytes 1179656 | tf_op jit(solution)/shard_map/ppermute | solution.py:174
  59.1 15.4 %collective-permute-start.4 = (f32[8,80,128]{2,1,0:T(8,128)S(1)}, f32[8,80,128]{2,1,0:T(8,128)S(1)}, u32[]{:S(2)}, u32[]{:S(2)}) collective-permute-start(f32[8,80,128]{2,1,0:T(8,128)S(1)} %fusion.2), channel_id=1, source_target_pairs={{0,32},{1,481},{2,34},{3,483},{4,36},{5,485},{6,38},{7,487},{8,40}... | collective-permute-start | bytes 983048 | tf_op jit(solution)/shard_map/ppermute | solution.py:165
  67.4 18.7 %collective-permute-start.9 = (f32[8,48,128]{2,1,0:T(8,128)S(1)}, f32[8,48,128]{2,1,0:T(8,128)S(1)}, u32[]{:S(2)}, u32[]{:S(2)}) collective-permute-start(f32[8,48,128]{2,1,0:T(8,128)S(1)} %constant_dynamic-slice_fusion.2), channel_id=1, source_target_pairs={{0,32},{1,481},{2,34},{3,483},{4,36},{5,485},{6,38},{7,487},{8,40}... | collective-permute-start | bytes 589832 | tf_op jit(solution)/shard_map/ppermute | solution.py:165
  74.7 16.8 %collective-permute-start.5 = (f32[4,80,128]{2,1,0:T(8,128)S(1)}, f32[4,80,128]{2,1,0:T(8,128)S(1)}, u32[]{:S(2)}, u32[]{:S(2)}) collective-permute-start(f32[4,80,128]{2,1,0:T(8,128)S(1)} %constant_dynamic-slice_fusion.4), channel_id=1, source_target_pairs={{0,64},{1,449},{2,66},{3,451},{4,68},{5,453},{6,70},{7,455},{8,72}... | collective-permute-start | bytes 491528 | tf_op jit(solution)/shard_map/ppermute | solution.py:165
  91.5 22.8 %collective-permute-start.11 = (f32[4,48,128]{2,1,0:T(8,128)S(1)}, f32[4,48,128]{2,1,0:T(8,128)S(1)}, u32[]{:S(2)}, u32[]{:S(2)}) collective-permute-start(f32[4,48,128]{2,1,0:T(8,128)S(1)} %constant_dynamic-slice_fusion.1), channel_id=1, source_target_pairs={{0,64},{1,449},{2,66},{3,451},{4,68},{5,453},{6,70},{7,455},{8,72}... | collective-permute-start | bytes 294920 | tf_op jit(solution)/shard_map/ppermute | solution.py:165
  97.6 30.5 %collective-permute-start.6 = (f32[1,80,128]{2,1,0:T(8,128)S(1)}, f32[1,80,128]{2,1,0:T(8,128)S(1)}, u32[]{:S(2)}, u32[]{:S(2)}) collective-permute-start(f32[1,80,128]{2,1,0:T(8,128)S(1)} %constant_dynamic-slice_fusion.3), channel_id=1, source_target_pairs={{0,128},{1,385},{2,130},{3,387},{4,132},{5,389},{6,134},{7,391},{8... | collective-permute-start | bytes 122888 | tf_op jit(solution)/shard_map/ppermute | solution.py:165
  114.4 15.2 %collective-permute-start.12 = (f32[1,48,128]{2,1,0:T(8,128)S(1)}, f32[1,48,128]{2,1,0:T(8,128)S(1)}, u32[]{:S(2)}, u32[]{:S(2)}) collective-permute-start(f32[1,48,128]{2,1,0:T(8,128)S(1)} %constant_dynamic-slice_fusion), channel_id=1, source_target_pairs={{0,128},{1,385},{2,130},{3,387},{4,132},{5,389},{6,134},{7,391},{8... | collective-permute-start | bytes 73736 | tf_op jit(solution)/shard_map/ppermute | solution.py:165
  129.6 16.5 %collective-permute-start.13 = (f32[1,128,128]{2,1,0:T(8,128)S(1)}, f32[1,128,128]{2,1,0:T(8,128)S(1)}, u32[]{:S(2)}, u32[]{:S(2)}) collective-permute-start(f32[1,128,128]{2,1,0:T(8,128)S(1)} %get-tuple-element.26), channel_id=1, source_target_pairs={{0,128},{1,385},{2,130},{3,387},{4,132},{5,389},{6,134},{7,391},{8... | collective-permute-start | bytes 196616 | tf_op jit(solution)/shard_map/ppermute | solution.py:165
  142.6 16.4 %collective-permute-start.14 = (f32[1,128,128]{2,1,0:T(8,128)S(1)}, f32[1,128,128]{2,1,0:T(8,128)S(1)}, u32[]{:S(2)}, u32[]{:S(2)}) collective-permute-start(f32[1,128,128]{2,1,0:T(8,128)S(1)} %get-tuple-element.27), channel_id=1, source_target_pairs={{0,384},{1,129},{2,386},{3,131},{4,388},{5,133},{6,390},{7,135},{8... | collective-permute-start | bytes 196616 | tf_op jit(solution)/shard_map/ppermute | solution.py:165
Sparse Core Ops, SparseCore 0:
  25.9 51.0 reduce-scatter.2
  86.2 37.5 reduce-scatter.4
